TPU v7x, 256 devices: a whole 4x4x8 slice. The times are simulated.
256 devices in a mesh: expert: 32 (over z, x), replica: 4 (over y), section: 2 (over core).
Axes of the slice: x: 4, y: 4, z: 8, core: 2. Of those that a mesh axis runs over, the one named last changes fastest.
Arguments:
- frames: bfloat16 [2, 16384, 1024], P('section', ('expert', 'replica')), may hold values from -6 to 6
- cotangent: bfloat16 [2, 16384, 1024], P('section', ('expert', 'replica')), may hold values from -3 to 3
- expert_ids: int32 [2, 16384, 8], P('section', ('expert', 'replica')), may hold values from 0 to 63, all different within a row; in each aligned block of 128 rows (0 to 127, 128 to 255, ..., all dimensions but the last counted through in order) at most 24 rows name the same one
- gate_weights: float32 [2, 16384, 8], P('section', ('expert', 'replica')), may hold values from 0.05 to 1
- weight_in: bfloat16 [2, 64, 1024, 768], P('section', 'expert', 'replica'), may hold values from -0.1875 to 0.1875
- weight_out: bfloat16 [2, 64, 768, 1024], P('section', 'expert', None, 'replica'), may hold values from -0.21875 to 0.21875
Outputs:
- sent_grads: bfloat16 [2, 16384, 1024], P('section', ('expert', 'replica'))
- grad_in: bfloat16 [2, 64, 1024, 768], P('section', 'expert', 'replica')
- grad_out: bfloat16 [2, 64, 768, 1024], P('section', 'expert', None, 'replica')
Inputs may be any that keep to these rules, and one draw needn't show every extreme that they name: `expert_ids`: each row names 8 different experts; among the rows of one device no expert is named more than 24 times, a bound that some block reaches.
All inputs are finite; a program needn't handle non-finite values.
Results may differ from a plain program's by a relative error of at most 0.012.
Values may be sent and summed in bfloat16 or wider, within the bound.
A program may use at most 64 MiB of HBM per device.

v0:
```python
import jax
import jax.numpy as jnp
from jax import lax
from jax.sharding import PartitionSpec as P


def shifted(block, axis, distance):
    devices = range(lax.axis_size(axis))
    route = [((i - distance) % len(devices), i) for i in devices]
    return lax.ppermute(block, axis, route)


def silu_slope(value):
    sigma = jax.nn.sigmoid(value)
    return sigma * (1.0 + value * (1.0 - sigma))


def per_device(frames, cotangent, expert_ids, gate_weights, weight_in, weight_out):
    expert_count = lax.axis_size("expert")
    local_experts = weight_in.shape[1]
    all_experts = local_experts * expert_count
    frame_count = frames.shape[1]
    model_width = frames.shape[2]
    choose_count = expert_ids.shape[2]
    capacity = max(frame_count * 3 // 16, frame_count * choose_count // all_experts)
    flat_ids = expert_ids[0].reshape(-1)
    flat_gate = gate_weights[0].reshape(-1)
    onehot = (flat_ids[:, None] == jnp.arange(all_experts, dtype=jnp.int32)[None, :]).astype(
        jnp.int32
    )
    position = jnp.sum((jnp.cumsum(onehot, 0) - 1) * onehot, 1)
    slot_index = flat_ids * capacity + position
    token_index = jnp.arange(frame_count * choose_count, dtype=jnp.int32) // choose_count
    rows_x = frames[0][token_index]
    rows_g = (flat_gate[:, None] * cotangent[0][token_index].astype(jnp.float32)).astype(
        jnp.bfloat16
    )
    empty = jnp.zeros((all_experts * capacity, model_width), jnp.bfloat16)
    send_x = (
        empty.at[slot_index].set(rows_x).reshape(expert_count, local_experts, capacity, model_width)
    )
    send_g = (
        empty.at[slot_index].set(rows_g).reshape(expert_count, local_experts, capacity, model_width)
    )
    recv_x, recv_g = (
        lax.all_to_all(send_x, "expert", split_axis=0, concat_axis=0, tiled=True),
        lax.all_to_all(send_g, "expert", split_axis=0, concat_axis=0, tiled=True),
    )
    full_in, full_out = (
        lax.all_gather(weight_in, "replica", axis=2, tiled=True),
        lax.all_gather(weight_out, "replica", axis=3, tiled=True),
    )
    row_count = expert_count * capacity
    hidden_list = []
    pregrad_list = []
    rowgrad_list = []
    for member in range(local_experts):
        inputs_x = recv_x[:, member].reshape(row_count, model_width)
        slot_grad = recv_g[:, member].reshape(row_count, model_width)
        w_first = full_in[0, member]
        w_second = full_out[0, member]
        pre = jnp.dot(inputs_x, w_first, preferred_element_type=jnp.float32)
        hidden = jax.nn.silu(pre).astype(jnp.bfloat16)
        hidden_grad = lax.dot_general(
            slot_grad, w_second, (((1,), (1,)), ((), ())), preferred_element_type=jnp.float32
        )
        pre_grad = (hidden_grad * silu_slope(pre)).astype(jnp.bfloat16)
        row_grad = lax.dot_general(
            pre_grad, w_first, (((1,), (1,)), ((), ())), preferred_element_type=jnp.float32
        )
        hidden_list.append(hidden)
        pregrad_list.append(pre_grad)
        rowgrad_list.append(
            row_grad.astype(jnp.bfloat16).reshape(expert_count, capacity, model_width)
        )
    returned = jnp.stack(rowgrad_list, 1)
    back = lax.all_to_all(returned, "expert", split_axis=0, concat_axis=0, tiled=True)
    back_rows = back.reshape(all_experts * capacity, model_width)[slot_index]
    summed = jnp.sum(
        back_rows.reshape(frame_count, choose_count, model_width).astype(jnp.float32), 1
    )
    sent_grads = shifted(summed.astype(jnp.bfloat16)[None], "section", 1)
    hidden_all = jnp.stack(hidden_list, 0)
    pregrad_all = jnp.stack(pregrad_list, 0)
    in_list = []
    out_list = []
    for member in range(local_experts):
        inputs_x = recv_x[:, member].reshape(row_count, model_width)
        slot_grad = recv_g[:, member].reshape(row_count, model_width)
        in_list.append(
            lax.dot_general(
                inputs_x,
                pregrad_all[member],
                (((0,), (0,)), ((), ())),
                preferred_element_type=jnp.float32,
            )
        )
        out_list.append(
            lax.dot_general(
                hidden_all[member],
                slot_grad,
                (((0,), (0,)), ((), ())),
                preferred_element_type=jnp.float32,
            )
        )
    terms_in = jnp.stack(in_list, 0)[None]
    terms_out = jnp.stack(out_list, 0)[None]
    summed_in, summed_out = (
        lax.psum_scatter(
            terms_in.astype(jnp.bfloat16), "replica", scatter_dimension=2, tiled=True
        ).astype(jnp.float32),
        lax.psum_scatter(
            terms_out.astype(jnp.bfloat16), "replica", scatter_dimension=3, tiled=True
        ).astype(jnp.float32),
    )
    grad_in = summed_in.astype(jnp.bfloat16)
    grad_out = summed_out.astype(jnp.bfloat16)
    return (sent_grads, grad_in, grad_out)


def solution(mesh):
    placed = (
        P("section", ("expert", "replica"), None),
        P("section", ("expert", "replica"), None),
        P("section", ("expert", "replica"), None),
        P("section", ("expert", "replica"), None),
        P("section", "expert", "replica", None),
        P("section", "expert", None, "replica"),
    )
    return jax.shard_map(
        per_device,
        mesh=mesh,
        in_specs=placed,
        out_specs=(
            P("section", ("expert", "replica"), None),
            P("section", "expert", "replica", None),
            P("section", "expert", None, "replica"),
        ),
        check_vma=False,
    )
```

profile of v0, /device:TPU:1, one launch (start us, length us, event | category | flops | bytes accessed | tf_op | source)
XLA Modules:
  0.0 327.4 jit_solution(2914036886152003588)
XLA Ops:
  7.2 0.7 broadcast_multiply_fusion
  7.9 0.8 copy.18
  8.7 0.1 eq.29
  8.8 0.1 eq.25
  8.9 0.1 copy.17
  9.0 0.1 mul.56
  9.1 0.8 copy.22
  9.9 0.1 mul.58
  10.0 18.0 %reduce-window.6 = s32[64,8,128]{2,1,0:T(8,128)S(1)} reduce-window(s32[64,8,128]{2,1,0:T(8,128)S(1)} %fusion.16, s32[]{:T(128)} %constant.33.clone.1), window={size=1x1x128 pad=0_0x0_0x127_0}, to_apply=%region_0.0 | reduce-window | flops 8323072 | bytes 524292 | tf_op jit(solution)/shard_map/reduce-window
  28.0 0.1 slice.50
  28.2 0.1 copy.20
  28.4 0.1 add_add_fusion
  28.7 15.1 %scatter_custom_fusion = bf16[1536,1024]{1,0:T(8,128)(2,1)} fusion(s32[1024]{0:T(1024)S(1)} %bitcast.89, f32[1024]{0:T(1024)S(1)} %mul.58, bf16[]{:T(256)} %constant.31.clone.1, bf16[128,1024]{1,0:T(8,128)(2,1)S(1)} %bitcast.71, s32[1024]{0:T(1024)S(1)} %broadcast_clamp_fusion.1), kind=kCustom, calls=%fused_computation.15 | custom fusion | flops 3145728 | bytes 3416066 | tf_op jit(solution)/shard_map/scatter | solution.py:43
  43.7 11.9 %all-to-all-start = ((bf16[32,2,24,1024]{3,2,1,0:T(8,128)(2,1)}), bf16[32,2,24,1024]{3,2,1,0:T(8,128)(2,1)S(1)}, u32[]{:S(2)}, u32[]{:S(2)}) async-start(bf16[32,2,24,1024]{3,2,1,0:T(8,128)(2,1)} %bitcast.74), calls=%async_computation | async-start | bytes 6291456 | tf_op jit(solution)/shard_map/all_to_all | solution.py:47
  55.6 0.2 all-gather.5.cloned.1.call-start
  55.8 0.5 all-gather.5.cloned.1.call-update
  56.4 16.8 %scatter_custom_fusion.1 = bf16[1536,1024]{1,0:T(8,128)(2,1)} fusion(s32[1024]{0:T(1024)S(1)} %bitcast.90, bf16[128,1024]{1,0:T(8,128)(2,1)} %bitcast.93, s32[1024]{0:T(1024)S(1)} %broadcast_clamp_fusion.1, bf16[]{:T(256)} %constant.31.clone.1), kind=kCustom, calls=%fused_computation.17 | custom fusion | bytes 3146240 | tf_op jit(solution)/shard_map/scatter | solution.py:40
  73.2 52.8 %all-to-all-done = bf16[32,2,24,1024]{3,2,1,0:T(8,128)(2,1)S(1)} async-done(((bf16[32,2,24,1024]{3,2,1,0:T(8,128)(2,1)}), bf16[32,2,24,1024]{3,2,1,0:T(8,128)(2,1)S(1)}, u32[]{:S(2)}, u32[]{:S(2)}) %all-to-all-start) | async-done | bytes 3145760 | tf_op jit(solution)/shard_map/all_to_all | solution.py:47
  125.9 8.0 %all-to-all-start.1 = ((bf16[32,2,24,1024]{3,2,1,0:T(8,128)(2,1)}), bf16[32,2,24,1024]{3,2,1,0:T(8,128)(2,1)}, u32[]{:S(2)}, u32[]{:S(2)}) async-start(bf16[32,2,24,1024]{3,2,1,0:T(8,128)(2,1)} %bitcast.73), calls=%async_computation.1 | async-start | bytes 6291456 | tf_op jit(solution)/shard_map/all_to_all | solution.py:46
  134.0 0.7 all-gather.3.cloned.1.call-update
  134.7 0.3 reduce-scatter.5.cloned.1.call-start
  135.0 2.0 fusion.20
  137.0 67.5 %all-to-all-done.1 = bf16[32,2,24,1024]{3,2,1,0:T(8,128)(2,1)} async-done(((bf16[32,2,24,1024]{3,2,1,0:T(8,128)(2,1)}), bf16[32,2,24,1024]{3,2,1,0:T(8,128)(2,1)}, u32[]{:S(2)}, u32[]{:S(2)}) %all-to-all-start.1) | async-done | bytes 3145760 | tf_op jit(solution)/shard_map/all_to_all | solution.py:46
  204.6 2.2 fusion.21
  206.8 3.9 %fusion.11 = f32[768,768]{1,0:T(8,128)S(1)} fusion(bf16[768,1024]{1,0:T(8,128)(2,1)S(1)} %bitcast.77, bf16[1,2,1024,768]{3,2,1,0:T(8,128)(2,1)} %all-gather.5.cloned.1.call-done), kind=kOutput, calls=%fused_computation.37 | convolution fusion | flops 1207959552 | bytes 5505024 | tf_op jit(solution)/shard_map/dot_general | solution.py:62
  210.8 1.4 fusion.10
  212.2 0.8 copy-done.5
  213.0 1.5 fusion.9
  214.6 1.5 fusion.8
  216.1 1.9 pad_maximum_fusion.2
  218.1 4.0 %multiply_convert_fusion.3 = bf16[768,768]{1,0:T(8,128)(2,1)S(1)} fusion(f32[768,768]{1,0:T(8,128)} %copy-done.11, bf16[768,1024]{1,0:T(8,128)(2,1)S(1)} %bitcast.82, bf16[1,2,768,1024]{3,2,1,0:T(8,128)(2,1)} %all-gather.3.cloned.1.call-done), kind=kOutput, calls=%fused_computation.11 | convolution fusion | flops 1213267968 | bytes 6684672 | tf_op jit(solution)/shard_map/dot_general | solution.py:64
  222.2 1.4 convolution_convert_fusion.4
  223.6 0.9 copy-done.8
  224.5 0.7 copy-done.10
  225.2 1.8 multiply_convert_fusion.4
  227.0 1.4 convolution_convert_fusion.5
  228.4 1.9 pad_maximum_fusion
  230.3 7.0 %all-to-all-start.2 = ((bf16[32,2,24,1024]{3,2,1,0:T(8,128)(2,1)}), bf16[32,2,24,1024]{3,2,1,0:T(8,128)(2,1)S(1)}, u32[]{:S(2)}, u32[]{:S(2)}) async-start(bf16[32,2,24,1024]{3,2,1,0:T(8,128)(2,1)} %pad_maximum_fusion), calls=%async_computation.2 | async-start | bytes 6291456 | tf_op jit(solution)/shard_map/all_to_all | solution.py:77
  237.3 0.3 reduce-scatter.3.cloned.1.call-start
  237.6 3.4 %fusion.7 = bf16[1,1,1024,768]{3,2,1,0:T(8,128)(2,1)S(1)} fusion(bf16[768,1024]{1,0:T(8,128)(2,1)} %bitcast.78, bf16[768,768]{1,0:T(8,128)(2,1)} %copy-done.12), kind=kOutput, calls=%fused_computation.33 | convolution fusion | flops 1208745984 | bytes 4325376 | tf_op jit(solution)/shard_map/dot_general | solution.py:91
  241.0 1.4 fusion.6
  242.5 2.0 pad_maximum_fusion.1
  244.5 62.8 %all-to-all-done.2 = bf16[32,2,24,1024]{3,2,1,0:T(8,128)(2,1)S(1)} async-done(((bf16[32,2,24,1024]{3,2,1,0:T(8,128)(2,1)}), bf16[32,2,24,1024]{3,2,1,0:T(8,128)(2,1)S(1)}, u32[]{:S(2)}, u32[]{:S(2)}) %all-to-all-start.2) | async-done | bytes 3145760 | tf_op jit(solution)/shard_map/all_to_all | solution.py:77
  307.3 5.4 %gather_fusion = bf16[1024,1024]{1,0:T(8,128)(2,1)} fusion(bf16[1536,1024]{1,0:T(8,128)(2,1)S(1)} %bitcast.72, s32[1024]{0:T(1024)S(1)} %broadcast_clamp_fusion), kind=kCustom, calls=%fused_computation.2 | custom fusion | bytes 4198400 | tf_op jit(solution)/shard_map/gather | solution.py:78
  312.7 3.0 bitcast_reduce_fusion
  315.7 3.3 %collective-permute-start = (bf16[1,128,1024]{2,1,0:T(8,128)(2,1)S(1)}, bf16[1,128,1024]{2,1,0:T(8,128)(2,1)S(1)}, u32[]{:S(2)}, u32[]{:S(2)}) collective-permute-start(bf16[1,128,1024]{2,1,0:T(8,128)(2,1)S(1)} %bitcast.86), channel_id=1, source_target_pairs={{1,0},{0,1},{3,2},{2,3},{5,4},{4,5},{7,6},{6,7},{9,8},{8,9},{11,10... | collective-permute-start | bytes 786440 | tf_op jit(solution)/shard_map/ppermute | solution.py:10
  319.0 1.2 collective-permute-done
  320.2 0.7 copy.28
  (43 shorter events, 0.4 us)
Async XLA Ops:
  7.2 21.5 %copy-start = (bf16[1,128,1024]{2,1,0:T(8,128)(2,1)S(1)}, bf16[1,128,1024]{2,1,0:T(8,128)(2,1)}, u32[]{:S(2)}) copy-start(bf16[1,128,1024]{2,1,0:T(8,128)(2,1)} %param.7) | copy-start | bytes 786436
  43.7 82.2 %all-to-all-start = ((bf16[32,2,24,1024]{3,2,1,0:T(8,128)(2,1)}), bf16[32,2,24,1024]{3,2,1,0:T(8,128)(2,1)S(1)}, u32[]{:S(2)}, u32[]{:S(2)}) async-start(bf16[32,2,24,1024]{3,2,1,0:T(8,128)(2,1)} %bitcast.74), calls=%async_computation | async-start | bytes 6291456 | tf_op jit(solution)/shard_map/all_to_all | solution.py:47
  55.6 151.2 %all-gather.5.cloned.1.call-start = ((), (), s32[]{:S(2)}) async-start(), calls=%async_computation.6 | async-start | bytes 3932160 | tf_op jit(solution)/shard_map/all_gather | solution.py:50
  125.9 78.6 %all-to-all-start.1 = ((bf16[32,2,24,1024]{3,2,1,0:T(8,128)(2,1)}), bf16[32,2,24,1024]{3,2,1,0:T(8,128)(2,1)}, u32[]{:S(2)}, u32[]{:S(2)}) async-start(bf16[32,2,24,1024]{3,2,1,0:T(8,128)(2,1)} %bitcast.73), calls=%async_computation.1 | async-start | bytes 6291456 | tf_op jit(solution)/shard_map/all_to_all | solution.py:46
  134.0 84.1 %all-gather.3.cloned.1.call-start = ((), (), s32[]{:S(2)}) async-start(), calls=%async_computation.5 | async-start | bytes 3932160 | tf_op jit(solution)/shard_map/all_gather | solution.py:51
  134.7 185.5 %reduce-scatter.5.cloned.1.call-start = ((), (), s32[]{:S(2)}) async-start(), calls=%async_computation.8 | async-start | bytes 3932160 | tf_op jit(solution)/shard_map/reduce_scatter | solution.py:112
  206.8 4.0 %copy-start.3 = (bf16[32,1,24,1024]{3,2,1,0:T(8,128)(2,1)}, bf16[32,1,24,1024]{3,2,1,0:T(8,128)(2,1)S(1)}, u32[]{:S(2)}) copy-start(bf16[32,1,24,1024]{3,2,1,0:T(8,128)(2,1)S(1)} %get-tuple-element.6) | copy-start | bytes 4718596
  206.8 4.0 %copy-start.1 = (bf16[32,1,24,1024]{3,2,1,0:T(8,128)(2,1)}, bf16[32,1,24,1024]{3,2,1,0:T(8,128)(2,1)S(1)}, u32[]{:S(2)}) copy-start(bf16[32,1,24,1024]{3,2,1,0:T(8,128)(2,1)S(1)} %get-tuple-element.5) | copy-start | bytes 4718596
  206.8 4.0 %copy-start.6 = (bf16[1,2,1024,768]{3,2,1,0:T(8,128)(2,1)S(1)}, bf16[1,2,1024,768]{3,2,1,0:T(8,128)(2,1)}, u32[]{:S(2)}) copy-start(bf16[1,2,1024,768]{3,2,1,0:T(8,128)(2,1)} %all-gather.5.cloned.1.call-done) | copy-start | bytes 9437188
  210.8 1.5 copy-start.11
  210.8 2.3 copy-start.5
  212.2 2.3 copy-start.9
  213.0 1.5 copy-start.4
  218.1 4.1 %copy-start.7 = (bf16[1,2,1024,768]{3,2,1,0:T(8,128)(2,1)S(1)}, bf16[1,2,1024,768]{3,2,1,0:T(8,128)(2,1)}, u32[]{:S(2)}) copy-start(bf16[1,2,1024,768]{3,2,1,0:T(8,128)(2,1)} %all-gather.5.cloned.1.call-done) | copy-start | bytes 9437188
  222.1 1.5 copy-start.12
  222.1 2.3 copy-start.8
  222.1 3.0 copy-start.10
  227.0 1.4 copy-start.13
  230.3 77.0 %all-to-all-start.2 = ((bf16[32,2,24,1024]{3,2,1,0:T(8,128)(2,1)}), bf16[32,2,24,1024]{3,2,1,0:T(8,128)(2,1)S(1)}, u32[]{:S(2)}, u32[]{:S(2)}) async-start(bf16[32,2,24,1024]{3,2,1,0:T(8,128)(2,1)} %pad_maximum_fusion), calls=%async_computation.2 | async-start | bytes 6291456 | tf_op jit(solution)/shard_map/all_to_all | solution.py:77
  237.3 82.9 %reduce-scatter.3.cloned.1.call-start = ((), (), s32[]{:S(2)}) async-start(), calls=%async_computation.7 | async-start | bytes 3932160 | tf_op jit(solution)/shard_map/reduce_scatter | solution.py:109
  237.6 3.4 %copy-start.2 = (bf16[32,1,24,1024]{3,2,1,0:T(8,128)(2,1)S(1)}, bf16[32,1,24,1024]{3,2,1,0:T(8,128)(2,1)}, u32[]{:S(2)}) copy-start(bf16[32,1,24,1024]{3,2,1,0:T(8,128)(2,1)} %copy-done.1) | copy-start | bytes 4718596
  237.6 3.4 %copy-start.14 = (bf16[768,768]{1,0:T(8,128)(2,1)S(1)}, bf16[768,768]{1,0:T(8,128)(2,1)}, u32[]{:S(2)}) copy-start(bf16[768,768]{1,0:T(8,128)(2,1)} %copy-done.13) | copy-start | bytes 3538948
  315.7 4.5 %collective-permute-start = (bf16[1,128,1024]{2,1,0:T(8,128)(2,1)S(1)}, bf16[1,128,1024]{2,1,0:T(8,128)(2,1)S(1)}, u32[]{:S(2)}, u32[]{:S(2)}) collective-permute-start(bf16[1,128,1024]{2,1,0:T(8,128)(2,1)S(1)} %bitcast.86), channel_id=1, source_target_pairs={{1,0},{0,1},{3,2},{2,3},{5,4},{4,5},{7,6},{6,7},{9,8},{8,9},{11,10... | collective-permute-start | bytes 786440 | tf_op jit(solution)/shard_map/ppermute | solution.py:10
Sparse Core Ops, SparseCore 0:
  58.3 43.8 all-gather.4
  136.6 46.8 all-gather.2
  218.2 40.8 reduce-scatter.4
  262.1 40.5 reduce-scatter.2
where the time goes:
time: 328 us; the launch traced here: 327 us
  waiting for transfers between devices  186 us (57%)
  other arithmetic  43 us (13%)
  local copies, waits for them, and re-layouts  32 us (10%)
  starting transfers between devices  31 us (9%)
  matrix products  21.8 us (7%)
  between operations  14.2 us (4%)
    all_to_all x1, waiting for transfers between devices, per_device(): lax.all_to_all(send_x, 'expert', split_axis=0, concat_axis=0, tiled=True)  67.5 us
    all_to_all x1, waiting for transfers between devices, per_device(): lax.all_to_all(returned, 'expert', split_axis=0, concat_axis=0, tiled=True)  62.8 us
    all_to_all x1, waiting for transfers between devices, per_device(): lax.all_to_all(send_g, 'expert', split_axis=0, concat_axis=0, tiled=True)  52.8 us
    another operation x2, other arithmetic  18 us
    scatter x1, local copies, waits for them, and re-layouts, per_device(): empty.at[slot_index].set(rows_x)  16.8 us
    scatter x1, other arithmetic, per_device(): empty.at[slot_index].set(rows_g)  15.1 us
    all_to_all x1, starting transfers between devices, per_device(): lax.all_to_all(send_g, 'expert', split_axis=0, concat_axis=0, tiled=True)  11.9 us
    all_to_all x1, starting transfers between devices, per_device(): lax.all_to_all(send_x, 'expert', split_axis=0, concat_axis=0, tiled=True)  8.02 us
  transfers between devices with their start and end apart: 8, of which 4 were waited for; matrix products, arithmetic and copies ran while one was open for 17% of the time, Pallas kernels for 0%

commit v1 on v0

v1 whole, which is shorter than its diff:
```python
import jax
import jax.numpy as jnp
from jax import lax
from jax.experimental import pallas as pl
from jax.experimental.pallas import tpu as pltpu
from jax.sharding import PartitionSpec as P

MESH = pl.DeviceIdType.MESH
NZ, NX, NY = 8, 4, 4
FRAMES = 128
D, H = 1024, 768
MOST = 24
PAIR = 2 * MOST
LOCAL = 2
PLANE = NX * LOCAL
ROWS = NZ * NX * MOST
CHUNK = ROWS // 2
QUARTER = D // NY
TILE = 256
COPIES = 128
ORDER = (0, 1, 7, 2, 6, 3, 5, 4)
SLOT = {distance: place for place, distance in enumerate(ORDER)}
PAIRS = len(ORDER) // 2
F32, BF16 = jnp.float32, jnp.bfloat16


def contract(a, b, dim_a, dim_b):
    return lax.dot_general(a, b, (((dim_a,), (dim_b,)), ((), ())), preferred_element_type=F32)


def kernel(
    route_ref,
    x_ref,
    c_ref,
    wi_ref,
    wo_ref,
    sent_ref,
    gi_ref,
    go_ref,
    tok,
    rt,
    hot,
    xs,
    xr,
    wi,
    wo,
    hb,
    pb,
    rg,
    rr,
    par,
    zhalf,
    zin,
    pi,
    po,
    hop_i,
    hop_o,
    end_i,
    end_o,
    fin,
    send_sems,
    recv_sems,
    own_sems,
):
    expert = lax.axis_index("expert")
    z, x = expert // NX, expert % NX
    y, s = lax.axis_index("replica"), lax.axis_index("section")

    def device(dz, dx, dy):
        place = lax.rem(z + dz + NZ, NZ) * NX + lax.rem(x + dx + NX, NX)
        return place, lax.rem(y + dy + NY, NY), s

    z_up, z_down = device(1, 0, 0), device(-1, 0, 0)
    y_up, y_down = device(0, 0, 1), device(0, 0, -1)
    x_far = [device(0, d, 0) for d in range(NX)]
    partner = (expert, y, 1 - s)

    barrier = pltpu.get_barrier_semaphore()
    peers = [z_up, z_down, y_up, y_down, *x_far[1:], partner]
    for peer in peers:
        pl.semaphore_signal(barrier, inc=1, device_id=peer, device_id_type=MESH)
    tok[0, pl.ds(0, FRAMES), :] = x_ref[...]
    tok[1, pl.ds(0, FRAMES), :] = c_ref[...]
    rt[0] = route_ref[...]
    pl.semaphore_wait(barrier, len(peers))

    started = []

    def send(src, dst, to):
        number = len(started)
        copy = pltpu.make_async_remote_copy(
            src_ref=src,
            dst_ref=dst,
            send_sem=send_sems.at[number],
            recv_sem=recv_sems.at[number],
            device_id=to,
            device_id_type=MESH,
        )
        copy.start()
        started.append(copy)
        return copy

    def arrive(copies):
        for copy in copies:
            copy.wait_recv()

    def relay(distance, step, half=None):
        land = (distance + step) % NZ
        to = z_up if step < 0 else z_down
        a, b, size = SLOT[distance] * FRAMES, SLOT[land] * FRAMES, FRAMES
        if half is not None:
            size = FRAMES // 2
            a, b = a + half * size, b + half * size
        copies = []
        if half in (None, 0):
            copies.append(send(rt.at[SLOT[distance]], rt.at[SLOT[land]], to))
        copies.append(send(tok.at[:, pl.ds(a, size)], tok.at[:, pl.ds(b, size)], to))
        return copies

    y_next, y_last = lax.rem(y + 1, NY), lax.rem(y + NY - 1, NY)

    def gather_first(m):
        return [
            send(ref.at[m], full.at[m, y], to)
            for to in (y_up, y_down)
            for ref, full in ((wi_ref, wi), (wo_ref, wo))
        ]

    def gather_second(m, first):
        arrive(first)
        copies = []
        for full, size in ((wi, QUARTER // 2), (wo, H // 2)):
            for place, half, to in ((y_last, 0, y_up), (y_next, 1, y_down)):
                part = full.at[m, place, pl.ds(half * size, size)]
                copies.append(send(part, part, to))
        return copies

    up = relay(0, -1)
    down = relay(0, 1)
    first = [gather_first(m) for m in range(LOCAL)]
    own = []
    for m in range(LOCAL):
        for k, (ref, full) in enumerate(((wi_ref, wi), (wo_ref, wo))):
            own.append(pltpu.make_async_copy(ref.at[m], full.at[m, y], own_sems.at[m, k]))
            own[-1].start()

    earlier = (
        lax.broadcasted_iota(jnp.int32, (FRAMES, FRAMES), 0)
        < lax.broadcasted_iota(jnp.int32, (FRAMES, FRAMES), 1)
    ).astype(BF16)
    place_row = lax.broadcasted_iota(jnp.int32, (PAIR, 2 * FRAMES), 0).astype(F32)
    members = [
        (z * PLANE + lax.rem(x + q // LOCAL, NX) * LOCAL + q % LOCAL).astype(F32)
        for q in range(PLANE)
    ]

    def routing(slot):
        ids, gates = rt[slot, pl.ds(0, 8), :], rt[slot, pl.ds(8, 8), :]
        gate = jnp.concatenate(
            [
                jnp.sum(jnp.where(ids == member, gates, 0.0), 0, keepdims=True)
                for member in members
            ],
            0,
        )
        named = jnp.where(gate > 0.0, 1.0, 0.0)
        place = jnp.dot(named.astype(BF16), earlier, preferred_element_type=F32)
        return gate, jnp.where(gate > 0.0, place, -100.0)

    def pick(p):
        gate_a, place_a = routing(2 * p)
        gate_b, place_b = routing(2 * p + 1)
        gate = jnp.concatenate([gate_a, gate_b], 1)
        place = jnp.concatenate([place_a, place_b + float(MOST)], 1)
        slot_gates = []
        for q in range(PLANE):
            match = place_row == place[q : q + 1, :]
            hot[p, pl.ds(q * PAIR, PAIR), :] = jnp.where(match, 1.0, 0.0).astype(BF16)
            slot_gates.append(
                jnp.sum(jnp.where(match, gate[q : q + 1, :], 0.0), 1, keepdims=True)
            )
        slot_gate = jnp.concatenate(slot_gates, 0)
        source = pl.ds(p * 2 * FRAMES, 2 * FRAMES)
        for kind in range(2):
            for n in range(D // TILE):
                columns = pl.ds(n * TILE, TILE)
                rows = jnp.dot(hot[p], tok[kind, source, columns], preferred_element_type=F32)
                if kind:
                    rows = rows * slot_gate
                rows = rows.astype(BF16)
                for q in range(PLANE):
                    d, m = q // LOCAL, q % LOCAL
                    block = rows[q * PAIR : (q + 1) * PAIR, :]
                    if d:
                        xs[p, m, d - 1, kind, :, columns] = block
                    else:
                        xr[m, kind, pl.ds(p * NX * PAIR, PAIR), columns] = block

    def scatter(p, m):
        copies = []
        for d in range(1, NX):
            rows = pl.ds((p * NX + NX - d) * PAIR, PAIR)
            copies.append(send(xs.at[p, m, d - 1], xr.at[m, :, rows], x_far[d]))
        return copies

    rows_in = {}
    arrive(up)
    up = relay(7, -1)
    arrive(down)
    down = relay(1, 1)
    pick(0)
    rows_in[0, 0] = scatter(0, 0)
    rows_in[0, 1] = scatter(0, 1)
    arrive(up)
    up = relay(6, -1)
    arrive(down)
    down = relay(2, 1)
    pick(1)
    rows_in[1, 0] = scatter(1, 0)
    second = [gather_second(0, first[0])]
    arrive(up)
    up = relay(5, -1, 0)
    arrive(down)
    down = relay(3, 1, 1)
    pick(2)
    rows_in[2, 0] = scatter(2, 0)
    second.append(gather_second(1, first[1]))
    arrive(up)
    arrive(down)
    pick(3)
    rows_in[3, 0] = scatter(3, 0)
    for p in range(1, PAIRS):
        rows_in[p, 1] = scatter(p, 1)

    def forward(m, c):
        rows = pl.ds(c * CHUNK, CHUNK)

        @pl.loop(0, H // TILE)
        def _(n):
            columns = pl.ds(pl.multiple_of(n * TILE, TILE), TILE)
            pre = jnp.zeros((CHUNK, TILE), F32)
            hidden_grad = jnp.zeros((CHUNK, TILE), F32)
            for r in range(NY):
                part = pl.ds(r * QUARTER, QUARTER)
                pre += contract(xr[m, 0, rows, part], wi[m, r, :, columns], 1, 0)
                hidden_grad += contract(xr[m, 1, rows, part], wo[m, r, columns, :], 1, 1)
            sigma = jax.nn.sigmoid(pre)
            slope = sigma * (1.0 + pre * (1.0 - sigma))
            hb[columns, rows] = jnp.transpose(pre * sigma).astype(BF16)
            pb[rows, columns] = (hidden_grad * slope).astype(BF16)

    def backward(m, c):
        rows = pl.ds(c * CHUNK, CHUNK)

        @pl.loop(0, NY)
        def _(r):
            columns = pl.ds(pl.multiple_of(r * QUARTER, QUARTER), QUARTER)
            rg[m, rows, columns] = contract(pb[rows, :], wi[m, r], 1, 1).astype(BF16)

    def parts(m, j):
        columns = pl.ds(pl.multiple_of(lax.rem(y + j, NY) * QUARTER, QUARTER), QUARTER)
        pi[m, j] = contract(xr[m, 0, :, columns], pb[...], 0, 0).astype(BF16)
        po[m, j] = contract(hb[...], xr[m, 1, :, columns], 1, 0).astype(BF16)

    half_i, half_o = QUARTER // 2, H // 2

    def reduce_first(m):
        copies = []
        for way, to in ((0, y_up), (1, y_down)):
            copies.append(send(pi.at[m, 2, pl.ds(way * half_i, half_i)], hop_i.at[m, way], to))
            copies.append(send(po.at[m, 2, pl.ds(way * half_o, half_o)], hop_o.at[m, way], to))
        return copies

    def add(ref, place, term):
        ref[place] = (ref[place].astype(F32) + term.astype(F32)).astype(BF16)

    def reduce_second(m, copies):
        after = []
        for way, to in ((0, y_up), (1, y_down)):
            j = 1 if way == 0 else 3
            arrive(copies[2 * way : 2 * way + 2])
            add(pi, (m, j, pl.ds(way * half_i, half_i)), hop_i[m, way])
            add(po, (m, j, pl.ds(way * half_o, half_o)), hop_o[m, way])
            after.append(send(pi.at[m, j], end_i.at[m, way], to))
            after.append(send(po.at[m, j], end_o.at[m, way], to))
        return after

    def reduce_last(m, copies):
        arrive(copies)
        for out, part, end in ((gi_ref, pi, end_i), (go_ref, po, end_o)):
            total = part[m, 0].astype(F32) + end[m, 0].astype(F32) + end[m, 1].astype(F32)
            out[m] = total.astype(BF16)

    def rows_back(p, m):
        copies = []
        for b in range(1, NX):
            rows = pl.ds((p * NX + b) * PAIR, PAIR)
            place = pl.ds(((NX - b) * LOCAL + m) * PAIR, PAIR)
            copies.append(send(rg.at[m, rows], rr.at[p, place], x_far[b]))
        rr[p, pl.ds(m * PAIR, PAIR), :] = rg[m, pl.ds(p * NX * PAIR, PAIR), :]
        return copies

    def combine(p):
        for n in range(D // TILE):
            columns = pl.ds(n * TILE, TILE)
            total = contract(hot[p], rr[p, :, columns], 0, 0)
            par[pl.ds(p * 2 * FRAMES, 2 * FRAMES), columns] = total.astype(BF16)

    arrive(second[0])
    own[0].wait()
    own[1].wait()
    for c in range(2):
        for p in (2 * c, 2 * c + 1):
            arrive(rows_in[p, 0])
        forward(0, c)
    parts(0, 2)
    sums = [reduce_first(0)]
    parts(0, 1)
    parts(0, 3)
    parts(0, 0)
    for c in range(2):
        backward(0, c)
    sums[0] = reduce_second(0, sums[0])

    arrive(second[1])
    own[2].wait()
    own[3].wait()
    for c in range(2):
        for p in (2 * c, 2 * c + 1):
            arrive(rows_in[p, 1])
        if c == 1:
            back = {(p, 0): rows_back(p, 0) for p in reversed(range(PAIRS))}
        forward(1, c)
    parts(1, 2)
    sums.append(reduce_first(1))
    parts(1, 1)
    parts(1, 3)
    for c in (1, 0):
        backward(1, c)
        for p in (2 * c + 1, 2 * c):
            back[p, 1] = rows_back(p, 1)
    parts(1, 0)
    sums[1] = reduce_second(1, sums[1])
    reduce_last(0, sums[0])

    def chunk(distance, half=None):
        start, size = SLOT[distance] * FRAMES, FRAMES
        if half is not None:
            size = FRAMES // 2
            start += half * size
        return pl.ds(start, size)

    def returned(p):
        arrive(back[p, 0] + back[p, 1])
        combine(p)

    returned(3)
    up = send(par.at[chunk(4, 0)], zhalf.at[0], z_up)
    down = send(par.at[chunk(4, 1)], zhalf.at[1], z_down)
    returned(2)
    arrive([up])
    add(par, (chunk(3, 0),), zhalf[0])
    up = send(par.at[chunk(3)], zin.at[0, 0], z_up)
    arrive([down])
    add(par, (chunk(5, 1),), zhalf[1])
    down = send(par.at[chunk(5)], zin.at[1, 0], z_down)
    returned(1)
    for step, (a, b) in enumerate(((2, 6), (1, 7))):
        if step == 1:
            returned(0)
        arrive([up])
        add(par, (chunk(a),), zin[0, step])
        up = send(par.at[chunk(a)], zin.at[0, step + 1], z_up)
        arrive([down])
        add(par, (chunk(b),), zin[1, step])
        down = send(par.at[chunk(b)], zin.at[1, step + 1], z_down)
    arrive([up, down])
    total = par[chunk(0), :].astype(F32) + zin[0, 2].astype(F32) + zin[1, 2].astype(F32)
    fin[...] = total.astype(BF16)
    last = send(fin, sent_ref, partner)
    reduce_last(1, sums[1])
    arrive([last])
    for copy in started:
        copy.wait_send()


def per_device(frames, cotangent, expert_ids, gate_weights, weight_in, weight_out):
    route = jnp.concatenate([expert_ids[0].astype(F32).T, gate_weights[0].T], 0)
    vmem = pl.BlockSpec(memory_space=pltpu.VMEM)
    anywhere = pl.BlockSpec(memory_space=pl.ANY)
    sent, grad_in, grad_out = pl.pallas_call(
        kernel,
        name="relay",
        out_shape=(
            jax.ShapeDtypeStruct((FRAMES, D), BF16),
            jax.ShapeDtypeStruct((LOCAL, QUARTER, H), BF16),
            jax.ShapeDtypeStruct((LOCAL, H, QUARTER), BF16),
        ),
        in_specs=[vmem, vmem, vmem, anywhere, anywhere],
        out_specs=(anywhere, vmem, vmem),
        scratch_shapes=[
            pltpu.VMEM((2, NZ * FRAMES, D), BF16),
            pltpu.VMEM((NZ, 16, FRAMES), F32),
            pltpu.VMEM((PAIRS, PLANE * PAIR, 2 * FRAMES), BF16),
            pltpu.VMEM((PAIRS, LOCAL, NX - 1, 2, PAIR, D), BF16),
            pltpu.VMEM((LOCAL, 2, ROWS, D), BF16),
            pltpu.VMEM((LOCAL, NY, QUARTER, H), BF16),
            pltpu.VMEM((LOCAL, NY, H, QUARTER), BF16),
            pltpu.VMEM((H, ROWS), BF16),
            pltpu.VMEM((ROWS, H), BF16),
            pltpu.VMEM((LOCAL, ROWS, D), BF16),
            pltpu.VMEM((PAIRS, PLANE * PAIR, D), BF16),
            pltpu.VMEM((NZ * FRAMES, D), BF16),
            pltpu.VMEM((2, FRAMES // 2, D), BF16),
            pltpu.VMEM((2, 3, FRAMES, D), BF16),
            pltpu.VMEM((LOCAL, NY, QUARTER, H), BF16),
            pltpu.VMEM((LOCAL, NY, H, QUARTER), BF16),
            pltpu.VMEM((LOCAL, 2, QUARTER // 2, H), BF16),
            pltpu.VMEM((LOCAL, 2, H // 2, QUARTER), BF16),
            pltpu.VMEM((LOCAL, 2, QUARTER, H), BF16),
            pltpu.VMEM((LOCAL, 2, H, QUARTER), BF16),
            pltpu.VMEM((FRAMES, D), BF16),
            pltpu.SemaphoreType.DMA((COPIES,)),
            pltpu.SemaphoreType.DMA((COPIES,)),
            pltpu.SemaphoreType.DMA((LOCAL, 2)),
        ],
        compiler_params=pltpu.CompilerParams(
            collective_id=0, has_side_effects=True, vmem_limit_bytes=60 * 2**20
        ),
    )(route, frames[0], cotangent[0], weight_in[0], weight_out[0])
    return sent[None], grad_in[None], grad_out[None]


def solution(mesh):
    rows = P("section", ("expert", "replica"), None)
    first = P("section", "expert", "replica", None)
    second = P("section", "expert", None, "replica")
    return jax.shard_map(
        per_device,
        mesh=mesh,
        in_specs=(rows, rows, rows, rows, first, second),
        out_specs=(rows, first, second),
        check_vma=False,
    )
```

time: 328 us -> 158 us (0.48)
  waiting for transfers between devices: 186 us -> 0 us
  Pallas kernels: 0 us -> 151 us
  other arithmetic: 43 us -> 0.6 us
  starting transfers between devices: 31 us -> 0 us
  local copies, waits for them, and re-layouts: 32 us -> 6.05 us
  matrix products: 21.8 us -> 0 us
  between operations: 14.2 us -> 0.65 us
    all_to_all x3 -> x0, waiting for transfers between devices: 183 us -> none  [the longest x1 67.5 us: per_device(): lax.all_to_all(send_x, 'expert', split_axis=0, concat_axis=0, tiled=True)]
    pallas_call x0 -> x1, Pallas kernels: none -> 151 us  [per_device(): pl.pallas_call(kernel, name='relay', out_shape=(jax.ShapeDtypeStruct((FRA...]
    all_to_all x3 -> x0, starting transfers between devices: 26.8 us -> none  [the longest x1 11.9 us: per_device(): lax.all_to_all(send_g, 'expert', split_axis=0, concat_axis=0, tiled=True)]
    another operation x5 -> x0, other arithmetic: 23.9 us -> none
    dot_general x10 -> x0, matrix products: 21.8 us -> none  [the longest x2 5.81 us: per_device(): lax.dot_general(slot_grad, w_second, (((1,), (1,)), ((), ())), preferred_...]
    scatter x1 -> x0, local copies, waits for them, and re-layouts: 16.8 us -> none  [per_device(): empty.at[slot_index].set(rows_x)]
    scatter x1 -> x0, other arithmetic: 15.1 us -> none  [per_device(): empty.at[slot_index].set(rows_g)]
    gather x1 -> x0, local copies, waits for them, and re-layouts: 5.39 us -> none  [per_device(): back_rows = back.reshape(all_experts * capacity, model_width)[slot_index]]
  transfers between devices with their start and end apart: 8 -> 0, of which waited for: 4 -> 0; matrix products, arithmetic and copies ran while one was open for 17% -> 0% of each run, Pallas kernels for 0% -> 0%
where the time goes in v1:
time: 158 us
  Pallas kernels  151 us (96%)
  local copies, waits for them, and re-layouts  6.05 us (4%)
    pallas_call x1, Pallas kernels, per_device(): pl.pallas_call(kernel, name='relay', out_shape=(jax.ShapeDtypeStruct((FRA...  151 us
    unnamed x9, local copies, waits for them, and re-layouts  6.05 us

profile of v1, /device:TPU:1, one launch (start us, length us, event | category | flops | bytes accessed | tf_op | source)
XLA Modules:
  0.0 158.0 jit_solution(17153184426083037955)
XLA Ops:
  0.6 0.0 copy-start.1
  0.6 0.7 copy-done.1
  1.3 0.0 copy-start.2
  1.3 0.7 copy-done.2
  2.0 0.6 pad_maximum_fusion.route_ref
  2.6 150.7 %relay.1 = (bf16[128,1024]{1,0:T(8,128)(2,1)}, bf16[2,256,768]{2,1,0:T(8,128)(2,1)}, bf16[2,768,256]{2,1,0:T(8,128)(2,1)}) custom-call(f32[16,128]{1,0:T(8,128)} %pad_maximum_fusion.route_ref, bf16[128,1024]{1,0:T(8,128)(2,1)} %bitcast.19, bf16[128,1024]{1,0:T(8,128)(2,1)} %bitcast.20, bf16[2,256,768]{2,1,0:T(8,128)(2,1)} %bitcast.16, ...), custom_call_target="tpu_custom_call" | custom-call | tf_op jit(solution)/shard_map/relay/pallas_call | solution.py:391
  153.3 1.7 %copy.12 = bf16[1,128,1024]{2,1,0:T(8,128)(2,1)} copy(bf16[1,128,1024]{2,1,0:T(8,128)(2,1)} %bitcast.18) | data formatting | bytes 524288
  154.9 0.0 copy-start
  154.9 2.1 %copy.13 = bf16[1,2,256,768]{3,2,1,0:T(8,128)(2,1)} copy(bf16[1,2,256,768]{3,2,1,0:T(8,128)(2,1)} %bitcast.15) | data formatting | bytes 1572864
  157.1 0.0 copy-done
  157.1 0.9 copy.14
  (1 shorter events, 0.0 us)
Async XLA Ops:
  0.6 0.7 copy-start.1
  1.3 0.7 copy-start.2
  154.9 2.1 %copy-start = (bf16[2,768,256]{2,1,0:T(8,128)(2,1)S(1)}, bf16[2,768,256]{2,1,0:T(8,128)(2,1)}, u32[]{:S(2)}) copy-start(bf16[2,768,256]{2,1,0:T(8,128)(2,1)} %get-tuple-element.8) | copy-start | bytes 2359300

commit v2 on v1

--- a/solution.py
+++ b/solution.py
@@ -17,7 +17,8 @@
 CHUNK = ROWS // 2
 QUARTER = D // NY
 TILE = 256
-COPIES = 128
+COPIES = 176
+HALVES = ((0, D // 2), (D // 2, D // 2))
 ORDER = (0, 1, 7, 2, 6, 3, 5, 4)
 SLOT = {distance: place for place, distance in enumerate(ORDER)}
 PAIRS = len(ORDER) // 2
@@ -29,7 +30,8 @@
 
 
 def kernel(
-    route_ref,
+    ids_ref,
+    gate_ref,
     x_ref,
     c_ref,
     wi_ref,
@@ -81,7 +83,8 @@
         pl.semaphore_signal(barrier, inc=1, device_id=peer, device_id_type=MESH)
     tok[0, pl.ds(0, FRAMES), :] = x_ref[...]
     tok[1, pl.ds(0, FRAMES), :] = c_ref[...]
-    rt[0] = route_ref[...]
+    rt[0, pl.ds(0, 8), :] = ids_ref[...].astype(F32)
+    rt[0, pl.ds(8, 8), :] = gate_ref[...]
     pl.semaphore_wait(barrier, len(peers))
 
     started = []
@@ -104,18 +107,19 @@
         for copy in copies:
             copy.wait_recv()
 
-    def relay(distance, step, half=None):
+    def hop_route(distance, step):
+        to = z_up if step < 0 else z_down
+        return [send(rt.at[SLOT[distance]], rt.at[SLOT[(distance + step) % NZ]], to)]
+
+    def hop(distance, step, kind, half=None, columns=(0, D)):
         land = (distance + step) % NZ
         to = z_up if step < 0 else z_down
         a, b, size = SLOT[distance] * FRAMES, SLOT[land] * FRAMES, FRAMES
         if half is not None:
             size = FRAMES // 2
             a, b = a + half * size, b + half * size
-        copies = []
-        if half in (None, 0):
-            copies.append(send(rt.at[SLOT[distance]], rt.at[SLOT[land]], to))
-        copies.append(send(tok.at[:, pl.ds(a, size)], tok.at[:, pl.ds(b, size)], to))
-        return copies
+        columns = pl.ds(*columns)
+        return [send(tok.at[kind, pl.ds(a, size), columns], tok.at[kind, pl.ds(b, size), columns], to)]
 
     y_next, y_last = lax.rem(y + 1, NY), lax.rem(y + NY - 1, NY)
 
@@ -135,9 +139,13 @@
                 copies.append(send(part, part, to))
         return copies
 
-    up = relay(0, -1)
-    down = relay(0, 1)
-    first = [gather_first(m) for m in range(LOCAL)]
+    up_route, down_route = hop_route(0, -1), hop_route(0, 1)
+    up, down = {}, {}
+    for kind in range(2):
+        for columns in HALVES:
+            down[kind, columns] = hop(0, 1, kind, None, columns)
+            up[kind, columns] = hop(0, -1, kind, None, columns)
+    first = [gather_first(0)]
     own = []
     for m in range(LOCAL):
         for k, (ref, full) in enumerate(((wi_ref, wi), (wo_ref, wo))):
@@ -167,7 +175,7 @@
         place = jnp.dot(named.astype(BF16), earlier, preferred_element_type=F32)
         return gate, jnp.where(gate > 0.0, place, -100.0)
 
-    def pick(p):
+    def prepare(p):
         gate_a, place_a = routing(2 * p)
         gate_b, place_b = routing(2 * p + 1)
         gate = jnp.concatenate([gate_a, gate_b], 1)
@@ -179,58 +187,80 @@
             slot_gates.append(
                 jnp.sum(jnp.where(match, gate[q : q + 1, :], 0.0), 1, keepdims=True)
             )
-        slot_gate = jnp.concatenate(slot_gates, 0)
+        return jnp.concatenate(slot_gates, 0)
+
+    def pick(p, kind, slot_gate, columns=(0, D)):
         source = pl.ds(p * 2 * FRAMES, 2 * FRAMES)
-        for kind in range(2):
-            for n in range(D // TILE):
-                columns = pl.ds(n * TILE, TILE)
-                rows = jnp.dot(hot[p], tok[kind, source, columns], preferred_element_type=F32)
-                if kind:
-                    rows = rows * slot_gate
-                rows = rows.astype(BF16)
-                for q in range(PLANE):
-                    d, m = q // LOCAL, q % LOCAL
-                    block = rows[q * PAIR : (q + 1) * PAIR, :]
-                    if d:
-                        xs[p, m, d - 1, kind, :, columns] = block
-                    else:
-                        xr[m, kind, pl.ds(p * NX * PAIR, PAIR), columns] = block
-
-    def scatter(p, m):
-        copies = []
+        for start in range(columns[0], columns[0] + columns[1], TILE):
+            tile = pl.ds(start, TILE)
+            rows = jnp.dot(hot[p], tok[kind, source, tile], preferred_element_type=F32)
+            if kind:
+                rows = rows * slot_gate
+            rows = rows.astype(BF16)
+            for q in range(PLANE):
+                d, m = q // LOCAL, q % LOCAL
+                block = rows[q * PAIR : (q + 1) * PAIR, :]
+                if d:
+                    xs[p, m, d - 1, kind, :, tile] = block
+                else:
+                    xr[m, kind, pl.ds(p * NX * PAIR, PAIR), tile] = block
+
+    rows_in = {(p, m): [] for p in range(PAIRS) for m in range(LOCAL)}
+
+    def scatter(p, m, kind, columns=(0, D)):
+        columns = pl.ds(*columns)
         for d in range(1, NX):
             rows = pl.ds((p * NX + NX - d) * PAIR, PAIR)
-            copies.append(send(xs.at[p, m, d - 1], xr.at[m, :, rows], x_far[d]))
-        return copies
-
-    rows_in = {}
-    arrive(up)
-    up = relay(7, -1)
-    arrive(down)
-    down = relay(1, 1)
-    pick(0)
-    rows_in[0, 0] = scatter(0, 0)
-    rows_in[0, 1] = scatter(0, 1)
-    arrive(up)
-    up = relay(6, -1)
-    arrive(down)
-    down = relay(2, 1)
-    pick(1)
-    rows_in[1, 0] = scatter(1, 0)
-    second = [gather_second(0, first[0])]
-    arrive(up)
-    up = relay(5, -1, 0)
-    arrive(down)
-    down = relay(3, 1, 1)
-    pick(2)
-    rows_in[2, 0] = scatter(2, 0)
-    second.append(gather_second(1, first[1]))
-    arrive(up)
-    arrive(down)
-    pick(3)
-    rows_in[3, 0] = scatter(3, 0)
+            rows_in[p, m].append(
+                send(xs.at[p, m, d - 1, kind, :, columns], xr.at[m, kind, rows, columns], x_far[d])
+            )
+
+    arrive(down_route)
+    down_route = hop_route(1, 1)
+    slot_gate = prepare(0)
+    arrive(up_route)
+    up_route = hop_route(7, -1)
+    up_next, down_next = {}, {}
+    for kind in range(2):
+        for place, columns in enumerate(HALVES):
+            arrive(down[kind, columns])
+            if place == len(HALVES) - 1:
+                down_next[kind] = hop(1, 1, kind)
+                for part in HALVES:
+                    arrive(up[kind, part])
+                up_next[kind] = hop(7, -1, kind)
+            pick(0, kind, slot_gate, columns)
+            for m in range(LOCAL):
+                scatter(0, m, kind, columns)
+    up, down = up_next, down_next
+    for p, (a, b) in ((1, (6, 2)), (2, (5, 3))):
+        if p == 2:
+            second = [gather_second(0, first[0])]
+            first.append(gather_first(1))
+        arrive(down_route)
+        arrive(up_route)
+        if p == 1:
+            down_route = hop_route(b, 1)
+        up_route = hop_route(a, -1)
+        slot_gate = prepare(p)
+        up_next, down_next = {}, {}
+        for kind in range(2):
+            arrive(down[kind])
+            down_next[kind] = hop(b, 1, kind, 1 if p == 2 else None)
+            arrive(up[kind])
+            up_next[kind] = hop(a, -1, kind, 0 if p == 2 else None)
+            pick(p, kind, slot_gate)
+            scatter(p, 0, kind)
+        up, down = up_next, down_next
+    arrive(up_route)
+    slot_gate = prepare(3)
+    for kind in range(2):
+        arrive(down[kind] + up[kind])
+        pick(3, kind, slot_gate)
+        scatter(3, 0, kind)
     for p in range(1, PAIRS):
-        rows_in[p, 1] = scatter(p, 1)
+        for kind in range(2):
+            scatter(p, 1, kind)
 
     def forward(m, c):
         rows = pl.ds(c * CHUNK, CHUNK)
@@ -291,20 +321,21 @@
             total = part[m, 0].astype(F32) + end[m, 0].astype(F32) + end[m, 1].astype(F32)
             out[m] = total.astype(BF16)
 
-    def rows_back(p, m):
-        copies = []
+    back = {(p, columns): [] for p in range(PAIRS) for columns in ((0, D), *HALVES)}
+
+    def rows_back(p, m, columns=(0, D)):
+        part = pl.ds(*columns)
         for b in range(1, NX):
             rows = pl.ds((p * NX + b) * PAIR, PAIR)
             place = pl.ds(((NX - b) * LOCAL + m) * PAIR, PAIR)
-            copies.append(send(rg.at[m, rows], rr.at[p, place], x_far[b]))
-        rr[p, pl.ds(m * PAIR, PAIR), :] = rg[m, pl.ds(p * NX * PAIR, PAIR), :]
-        return copies
-
-    def combine(p):
-        for n in range(D // TILE):
-            columns = pl.ds(n * TILE, TILE)
-            total = contract(hot[p], rr[p, :, columns], 0, 0)
-            par[pl.ds(p * 2 * FRAMES, 2 * FRAMES), columns] = total.astype(BF16)
+            back[p, columns].append(send(rg.at[m, rows, part], rr.at[p, place, part], x_far[b]))
+        rr[p, pl.ds(m * PAIR, PAIR), part] = rg[m, pl.ds(p * NX * PAIR, PAIR), part]
+
+    def combine(p, columns):
+        for start in range(columns[0], columns[0] + columns[1], TILE):
+            tile = pl.ds(start, TILE)
+            total = contract(hot[p], rr[p, :, tile], 0, 0)
+            par[pl.ds(p * 2 * FRAMES, 2 * FRAMES), tile] = total.astype(BF16)
 
     arrive(second[0])
     own[0].wait()
@@ -315,6 +346,7 @@
         forward(0, c)
     parts(0, 2)
     sums = [reduce_first(0)]
+    second.append(gather_second(1, first[1]))
     parts(0, 1)
     parts(0, 3)
     parts(0, 0)
@@ -325,22 +357,26 @@
     arrive(second[1])
     own[2].wait()
     own[3].wait()
-    for c in range(2):
-        for p in (2 * c, 2 * c + 1):
-            arrive(rows_in[p, 1])
-        if c == 1:
-            back = {(p, 0): rows_back(p, 0) for p in reversed(range(PAIRS))}
-        forward(1, c)
+    arrive(rows_in[0, 1] + rows_in[1, 1])
+    forward(1, 0)
+    backward(1, 0)
+    arrive(rows_in[2, 1] + rows_in[3, 1])
+    rows_back(3, 0)
+    rows_back(2, 0)
+    forward(1, 1)
     parts(1, 2)
     sums.append(reduce_first(1))
+    backward(1, 1)
+    rows_back(3, 1)
+    rows_back(2, 1)
+    rows_back(1, 0)
+    rows_back(1, 1)
+    for columns in HALVES:
+        for m in range(LOCAL):
+            rows_back(0, m, columns)
     parts(1, 1)
     parts(1, 3)
-    for c in (1, 0):
-        backward(1, c)
-        for p in (2 * c + 1, 2 * c):
-            back[p, 1] = rows_back(p, 1)
     parts(1, 0)
-    sums[1] = reduce_second(1, sums[1])
     reduce_last(0, sums[0])
 
     def chunk(distance, half=None):
@@ -350,13 +386,14 @@
             start += half * size
         return pl.ds(start, size)
 
-    def returned(p):
-        arrive(back[p, 0] + back[p, 1])
-        combine(p)
+    def returned(p, columns=(0, D)):
+        arrive(back[p, columns])
+        combine(p, columns)
 
     returned(3)
     up = send(par.at[chunk(4, 0)], zhalf.at[0], z_up)
     down = send(par.at[chunk(4, 1)], zhalf.at[1], z_down)
+    sums[1] = reduce_second(1, sums[1])
     returned(2)
     arrive([up])
     add(par, (chunk(3, 0),), zhalf[0])
@@ -365,38 +402,66 @@
     add(par, (chunk(5, 1),), zhalf[1])
     down = send(par.at[chunk(5)], zin.at[1, 0], z_down)
     returned(1)
-    for step, (a, b) in enumerate(((2, 6), (1, 7))):
-        if step == 1:
-            returned(0)
-        arrive([up])
-        add(par, (chunk(a),), zin[0, step])
-        up = send(par.at[chunk(a)], zin.at[0, step + 1], z_up)
-        arrive([down])
-        add(par, (chunk(b),), zin[1, step])
-        down = send(par.at[chunk(b)], zin.at[1, step + 1], z_down)
-    arrive([up, down])
-    total = par[chunk(0), :].astype(F32) + zin[0, 2].astype(F32) + zin[1, 2].astype(F32)
-    fin[...] = total.astype(BF16)
-    last = send(fin, sent_ref, partner)
+    arrive([up])
+    add(par, (chunk(2),), zin[0, 0])
+    up = send(par.at[chunk(2)], zin.at[0, 1], z_up)
+    arrive([down])
+    add(par, (chunk(6),), zin[1, 0])
+    down = send(par.at[chunk(6)], zin.at[1, 1], z_down)
+    ends = []
+    for place, columns in enumerate(HALVES):
+        part = pl.ds(*columns)
+        returned(0, columns)
+        if place == 0:
+            arrive([down, up])
+        add(par, (chunk(7), part), zin[1, 1, :, part])
+        ends.append([send(par.at[chunk(7), part], zin.at[1, 2, :, part], z_down)])
+        add(par, (chunk(1), part), zin[0, 1, :, part])
+        ends[-1].append(send(par.at[chunk(1), part], zin.at[0, 2, :, part], z_up))
+    last = []
+    for end, columns in zip(ends, HALVES):
+        part = pl.ds(*columns)
+        arrive(end)
+        total = par[chunk(0), part].astype(F32)
+        total = total + zin[0, 2, :, part].astype(F32) + zin[1, 2, :, part].astype(F32)
+        fin[:, part] = total.astype(BF16)
+        last.append(send(fin.at[:, part], sent_ref.at[:, part], partner))
     reduce_last(1, sums[1])
-    arrive([last])
+    arrive(last)
     for copy in started:
         copy.wait_send()
 
 
+def publish(sent_in, gi_in, go_in, sent_out, gi_out, go_out, sent_held, gi_held, go_held, sems):
+    trios = []
+    for m in range(LOCAL):
+        trios.append((gi_in.at[m], gi_held.at[m], gi_out.at[m]))
+        trios.append((go_in.at[m], go_held.at[m], go_out.at[m]))
+    trios.append((sent_in, sent_held, sent_out))
+    inward = [pltpu.make_async_copy(a, h, sems.at[0, i]) for i, (a, h, _) in enumerate(trios)]
+    outward = [pltpu.make_async_copy(h, b, sems.at[1, i]) for i, (_, h, b) in enumerate(trios)]
+    for copy in inward:
+        copy.start()
+    for arriving, leaving in zip(inward, outward):
+        arriving.wait()
+        leaving.start()
+    for copy in outward:
+        copy.wait()
+
+
 def per_device(frames, cotangent, expert_ids, gate_weights, weight_in, weight_out):
-    route = jnp.concatenate([expert_ids[0].astype(F32).T, gate_weights[0].T], 0)
     vmem = pl.BlockSpec(memory_space=pltpu.VMEM)
     anywhere = pl.BlockSpec(memory_space=pl.ANY)
-    sent, grad_in, grad_out = pl.pallas_call(
+    shapes = (
+        jax.ShapeDtypeStruct((FRAMES, D), BF16),
+        jax.ShapeDtypeStruct((LOCAL, QUARTER, H), BF16),
+        jax.ShapeDtypeStruct((LOCAL, H, QUARTER), BF16),
+    )
+    results = pl.pallas_call(
         kernel,
         name="relay",
-        out_shape=(
-            jax.ShapeDtypeStruct((FRAMES, D), BF16),
-            jax.ShapeDtypeStruct((LOCAL, QUARTER, H), BF16),
-            jax.ShapeDtypeStruct((LOCAL, H, QUARTER), BF16),
-        ),
-        in_specs=[vmem, vmem, vmem, anywhere, anywhere],
+        out_shape=shapes,
+        in_specs=[vmem, vmem, vmem, vmem, anywhere, anywhere],
         out_specs=(anywhere, vmem, vmem),
         scratch_shapes=[
             pltpu.VMEM((2, NZ * FRAMES, D), BF16),
@@ -427,7 +492,18 @@
         compiler_params=pltpu.CompilerParams(
             collective_id=0, has_side_effects=True, vmem_limit_bytes=60 * 2**20
         ),
-    )(route, frames[0], cotangent[0], weight_in[0], weight_out[0])
+    )(expert_ids[0].T, gate_weights[0].T, frames[0], cotangent[0], weight_in[0], weight_out[0])
+    sent, grad_in, grad_out = pl.pallas_call(
+        publish,
+        name="publish",
+        out_shape=shapes,
+        in_specs=[anywhere] * 3,
+        out_specs=(anywhere,) * 3,
+        scratch_shapes=[
+            *[pltpu.VMEM(shape.shape, shape.dtype) for shape in shapes],
+            pltpu.SemaphoreType.DMA((2, 1 + 2 * LOCAL)),
+        ],
+    )(*results)
     return sent[None], grad_in[None], grad_out[None]
 
 

time: 158 us -> 142 us (0.90)
  Pallas kernels: 151 us -> 141 us
  local copies, waits for them, and re-layouts: 6.05 us -> 0 us
    pallas_call x1 -> x2, Pallas kernels: 151 us -> 141 us  [the longest x1 138 us: per_device(): pl.pallas_call(kernel, name='relay', out_shape=shapes, in_specs=[vmem, vm...]
    unnamed x9 -> x0, local copies, waits for them, and re-layouts: 6.05 us -> none
where the time goes in v2:
time: 142 us; the launch traced here: 141 us
  Pallas kernels  141 us (99%)
    pallas_call x1, Pallas kernels, per_device(): pl.pallas_call(kernel, name='relay', out_shape=shapes, in_specs=[vmem, vm...  138 us

profile of v2, /device:TPU:1, one launch (start us, length us, event | category | flops | bytes accessed | tf_op | source)
XLA Modules:
  0.0 141.5 jit_solution(10826739027530238658)
XLA Ops:
  0.6 138.3 %relay.1 = (bf16[128,1024]{1,0:T(8,128)(2,1)}, bf16[2,256,768]{2,1,0:T(8,128)(2,1)}, bf16[2,768,256]{2,1,0:T(8,128)(2,1)}) custom-call(s32[8,128]{1,0:T(8,128)} %bitcast.17, f32[8,128]{1,0:T(8,128)} %bitcast.18, bf16[128,1024]{1,0:T(8,128)(2,1)} %bitcast.15, bf16[128,1024]{1,0:T(8,128)(2,1)} %bitcast.16, bf16[2,256,768]{2,1,0:T(8,128)(2,1)} %bitcast.13, ...), custom_call_target="tpu_custom_call" | custom-call | tf_op jit(solution)/shard_map/relay/pallas_call | solution.py:460
  139.0 2.3 %publish.1 = (bf16[128,1024]{1,0:T(8,128)(2,1)}, bf16[2,256,768]{2,1,0:T(8,128)(2,1)}, bf16[2,768,256]{2,1,0:T(8,128)(2,1)}) custom-call(bf16[128,1024]{1,0:T(8,128)(2,1)} %get-tuple-element.9.sent_in, bf16[2,256,768]{2,1,0:T(8,128)(2,1)} %get-tuple-element.10.gi_in, bf16[2,768,256]{2,1,0:T(8,128)(2,1)} %get-tuple-element.11.go_in), custom_call_target="tpu_custom_call" | custom-call | tf_op jit(solution)/shard_map/publish/pallas_call | solution.py:496

commit v3 on v2

--- a/solution.py
+++ b/solution.py
@@ -18,7 +18,7 @@
 QUARTER = D // NY
 TILE = 256
 COPIES = 176
-HALVES = ((0, D // 2), (D // 2, D // 2))
+EARLY = 16
 ORDER = (0, 1, 7, 2, 6, 3, 5, 4)
 SLOT = {distance: place for place, distance in enumerate(ORDER)}
 PAIRS = len(ORDER) // 2
@@ -60,9 +60,11 @@
     end_i,
     end_o,
     fin,
+    ids_held,
     send_sems,
     recv_sems,
     own_sems,
+    local_sems,
 ):
     expert = lax.axis_index("expert")
     z, x = expert // NX, expert % NX
@@ -77,15 +79,24 @@
     x_far = [device(0, d, 0) for d in range(NX)]
     partner = (expert, y, 1 - s)
 
+    z_up_other, z_down_other = (*z_up[:2], 1 - s), (*z_down[:2], 1 - s)
     barrier = pltpu.get_barrier_semaphore()
-    peers = [z_up, z_down, y_up, y_down, *x_far[1:], partner]
+    peers = [z_up, z_down, y_up, y_down, *x_far[1:], partner, z_up_other, z_down_other]
     for peer in peers:
         pl.semaphore_signal(barrier, inc=1, device_id=peer, device_id_type=MESH)
-    tok[0, pl.ds(0, FRAMES), :] = x_ref[...]
-    tok[1, pl.ds(0, FRAMES), :] = c_ref[...]
-    rt[0, pl.ds(0, 8), :] = ids_ref[...].astype(F32)
-    rt[0, pl.ds(8, 8), :] = gate_ref[...]
-    pl.semaphore_wait(barrier, len(peers))
+    inputs = [
+        pltpu.make_async_copy(src, dst, local_sems.at[i])
+        for i, (src, dst) in enumerate(
+            (
+                (ids_ref, ids_held),
+                (gate_ref, rt.at[0, pl.ds(8, 8)]),
+                (x_ref, tok.at[0, pl.ds(0, FRAMES)]),
+                (c_ref, tok.at[1, pl.ds(0, FRAMES)]),
+            )
+        )
+    ]
+    for copy in inputs:
+        copy.start()
 
     started = []
 
@@ -111,15 +122,14 @@
         to = z_up if step < 0 else z_down
         return [send(rt.at[SLOT[distance]], rt.at[SLOT[(distance + step) % NZ]], to)]
 
-    def hop(distance, step, kind, half=None, columns=(0, D)):
+    def hop(distance, step, kind, half=None):
         land = (distance + step) % NZ
         to = z_up if step < 0 else z_down
         a, b, size = SLOT[distance] * FRAMES, SLOT[land] * FRAMES, FRAMES
         if half is not None:
             size = FRAMES // 2
             a, b = a + half * size, b + half * size
-        columns = pl.ds(*columns)
-        return [send(tok.at[kind, pl.ds(a, size), columns], tok.at[kind, pl.ds(b, size), columns], to)]
+        return [send(tok.at[kind, pl.ds(a, size)], tok.at[kind, pl.ds(b, size)], to)]
 
     y_next, y_last = lax.rem(y + 1, NY), lax.rem(y + NY - 1, NY)
 
@@ -138,19 +148,6 @@
                 part = full.at[m, place, pl.ds(half * size, size)]
                 copies.append(send(part, part, to))
         return copies
-
-    up_route, down_route = hop_route(0, -1), hop_route(0, 1)
-    up, down = {}, {}
-    for kind in range(2):
-        for columns in HALVES:
-            down[kind, columns] = hop(0, 1, kind, None, columns)
-            up[kind, columns] = hop(0, -1, kind, None, columns)
-    first = [gather_first(0)]
-    own = []
-    for m in range(LOCAL):
-        for k, (ref, full) in enumerate(((wi_ref, wi), (wo_ref, wo))):
-            own.append(pltpu.make_async_copy(ref.at[m], full.at[m, y], own_sems.at[m, k]))
-            own[-1].start()
 
     earlier = (
         lax.broadcasted_iota(jnp.int32, (FRAMES, FRAMES), 0)
@@ -175,6 +172,37 @@
         place = jnp.dot(named.astype(BF16), earlier, preferred_element_type=F32)
         return gate, jnp.where(gate > 0.0, place, -100.0)
 
+    inputs[0].wait()
+    inputs[1].wait()
+    rt[0, pl.ds(0, 8), :] = ids_held[...].astype(F32)
+    own_gate, own_place = routing(0)
+    own_match = [
+        place_row[:EARLY, :FRAMES] == own_place[q : q + 1, :] for q in range(PLANE)
+    ]
+    own_hot = jnp.concatenate([jnp.where(match, 1.0, 0.0) for match in own_match], 0).astype(BF16)
+    own_gate = jnp.concatenate(
+        [
+            jnp.sum(jnp.where(match, own_gate[q : q + 1, :], 0.0), 1, keepdims=True)
+            for q, match in enumerate(own_match)
+        ],
+        0,
+    )
+    inputs[2].wait()
+    inputs[3].wait()
+    pl.semaphore_wait(barrier, len(peers))
+
+    down_route, up_route = hop_route(0, 1), hop_route(0, -1)
+    up, down = {}, {}
+    for kind in range(2):
+        down[kind] = hop(0, 1, kind)
+        up[kind] = hop(0, -1, kind)
+    first = [gather_first(0)]
+    own = []
+    for m in range(LOCAL):
+        for k, (ref, full) in enumerate(((wi_ref, wi), (wo_ref, wo))):
+            own.append(pltpu.make_async_copy(ref.at[m], full.at[m, y], own_sems.at[m, k]))
+            own[-1].start()
+
     def prepare(p):
         gate_a, place_a = routing(2 * p)
         gate_b, place_b = routing(2 * p + 1)
@@ -183,38 +211,50 @@
         slot_gates = []
         for q in range(PLANE):
             match = place_row == place[q : q + 1, :]
-            hot[p, pl.ds(q * PAIR, PAIR), :] = jnp.where(match, 1.0, 0.0).astype(BF16)
+            hot[p, q] = jnp.where(match, 1.0, 0.0).astype(BF16)
             slot_gates.append(
                 jnp.sum(jnp.where(match, gate[q : q + 1, :], 0.0), 1, keepdims=True)
             )
         return jnp.concatenate(slot_gates, 0)
 
-    def pick(p, kind, slot_gate, columns=(0, D)):
+    def store(p, kind, rows, height, low, high, tile):
+        for q in range(PLANE):
+            d, m = q // LOCAL, q % LOCAL
+            start = q * height + (low if height == PAIR else 0)
+            block = rows[start : start + high - low]
+            if d:
+                xs[p, m, d - 1, kind, low:high, tile] = block
+            else:
+                xr[m, kind, pl.ds(p * NX * PAIR + low, high - low), tile] = block
+
+    def pick(p, kind, slot_gate, low=0):
         source = pl.ds(p * 2 * FRAMES, 2 * FRAMES)
-        for start in range(columns[0], columns[0] + columns[1], TILE):
+        chosen = hot[p].reshape(PLANE * PAIR, 2 * FRAMES)
+        for start in range(0, D, TILE):
             tile = pl.ds(start, TILE)
-            rows = jnp.dot(hot[p], tok[kind, source, tile], preferred_element_type=F32)
+            rows = jnp.dot(chosen, tok[kind, source, tile], preferred_element_type=F32)
             if kind:
                 rows = rows * slot_gate
-            rows = rows.astype(BF16)
-            for q in range(PLANE):
-                d, m = q // LOCAL, q % LOCAL
-                block = rows[q * PAIR : (q + 1) * PAIR, :]
-                if d:
-                    xs[p, m, d - 1, kind, :, tile] = block
-                else:
-                    xr[m, kind, pl.ds(p * NX * PAIR, PAIR), tile] = block
+            store(p, kind, rows.astype(BF16), PAIR, low, PAIR, tile)
 
     rows_in = {(p, m): [] for p in range(PAIRS) for m in range(LOCAL)}
 
-    def scatter(p, m, kind, columns=(0, D)):
-        columns = pl.ds(*columns)
+    def scatter(p, m, kind, low=0, high=PAIR):
         for d in range(1, NX):
-            rows = pl.ds((p * NX + NX - d) * PAIR, PAIR)
-            rows_in[p, m].append(
-                send(xs.at[p, m, d - 1, kind, :, columns], xr.at[m, kind, rows, columns], x_far[d])
-            )
-
+            src = xs.at[p, m, d - 1, kind, pl.ds(low, high - low)]
+            rows = pl.ds((p * NX + NX - d) * PAIR + low, high - low)
+            rows_in[p, m].append(send(src, xr.at[m, kind, rows], x_far[d]))
+
+    for kind in range(2):
+        for start in range(0, D, TILE):
+            tile = pl.ds(start, TILE)
+            frames = tok[kind, pl.ds(0, FRAMES), tile]
+            rows = jnp.dot(own_hot, frames, preferred_element_type=F32)
+            if kind:
+                rows = rows * own_gate
+            store(0, kind, rows.astype(BF16), EARLY, 0, EARLY, tile)
+        for m in range(LOCAL):
+            scatter(0, m, kind, 0, EARLY)
     arrive(down_route)
     down_route = hop_route(1, 1)
     slot_gate = prepare(0)
@@ -222,16 +262,13 @@
     up_route = hop_route(7, -1)
     up_next, down_next = {}, {}
     for kind in range(2):
-        for place, columns in enumerate(HALVES):
-            arrive(down[kind, columns])
-            if place == len(HALVES) - 1:
-                down_next[kind] = hop(1, 1, kind)
-                for part in HALVES:
-                    arrive(up[kind, part])
-                up_next[kind] = hop(7, -1, kind)
-            pick(0, kind, slot_gate, columns)
-            for m in range(LOCAL):
-                scatter(0, m, kind, columns)
+        arrive(down[kind])
+        down_next[kind] = hop(1, 1, kind)
+        arrive(up[kind])
+        up_next[kind] = hop(7, -1, kind)
+        pick(0, kind, slot_gate, EARLY)
+        for m in range(LOCAL):
+            scatter(0, m, kind, EARLY)
     up, down = up_next, down_next
     for p, (a, b) in ((1, (6, 2)), (2, (5, 3))):
         if p == 2:
@@ -315,27 +352,34 @@
             after.append(send(po.at[m, j], end_o.at[m, way], to))
         return after
 
+    outputs = []
+
     def reduce_last(m, copies):
         arrive(copies)
-        for out, part, end in ((gi_ref, pi, end_i), (go_ref, po, end_o)):
+        for k, (out, part, end) in enumerate(((gi_ref, pi, end_i), (go_ref, po, end_o))):
             total = part[m, 0].astype(F32) + end[m, 0].astype(F32) + end[m, 1].astype(F32)
-            out[m] = total.astype(BF16)
-
-    back = {(p, columns): [] for p in range(PAIRS) for columns in ((0, D), *HALVES)}
-
-    def rows_back(p, m, columns=(0, D)):
-        part = pl.ds(*columns)
+            part[m, 0] = total.astype(BF16)
+            outputs.append(
+                pltpu.make_async_copy(part.at[m, 0], out.at[m], local_sems.at[4 + 2 * m + k])
+            )
+            outputs[-1].start()
+
+    back = {(p, low): [] for p in range(PAIRS) for low in (0, EARLY)}
+
+    def rows_back(p, m, low=0, high=PAIR):
         for b in range(1, NX):
-            rows = pl.ds((p * NX + b) * PAIR, PAIR)
-            place = pl.ds(((NX - b) * LOCAL + m) * PAIR, PAIR)
-            back[p, columns].append(send(rg.at[m, rows, part], rr.at[p, place, part], x_far[b]))
-        rr[p, pl.ds(m * PAIR, PAIR), part] = rg[m, pl.ds(p * NX * PAIR, PAIR), part]
-
-    def combine(p, columns):
-        for start in range(columns[0], columns[0] + columns[1], TILE):
+            rows = pl.ds((p * NX + b) * PAIR + low, high - low)
+            place = rr.at[p, (NX - b) * LOCAL + m, pl.ds(low, high - low)]
+            back[p, low].append(send(rg.at[m, rows], place, x_far[b]))
+        rr[p, m, low:high, :] = rg[m, pl.ds(p * NX * PAIR + low, high - low), :]
+
+    def combine(p, low, begin, end):
+        chosen = hot[p, :, low:, begin:end].reshape(PLANE * (PAIR - low), end - begin)
+        for start in range(0, D, TILE):
             tile = pl.ds(start, TILE)
-            total = contract(hot[p], rr[p, :, tile], 0, 0)
-            par[pl.ds(p * 2 * FRAMES, 2 * FRAMES), tile] = total.astype(BF16)
+            rows = rr[p, :, low:, tile].reshape(PLANE * (PAIR - low), TILE)
+            total = contract(chosen, rows, 0, 0)
+            par[pl.ds(p * 2 * FRAMES + begin, end - begin), tile] = total.astype(BF16)
 
     arrive(second[0])
     own[0].wait()
@@ -360,8 +404,9 @@
     arrive(rows_in[0, 1] + rows_in[1, 1])
     forward(1, 0)
     backward(1, 0)
-    arrive(rows_in[2, 1] + rows_in[3, 1])
+    arrive(rows_in[2, 1])
     rows_back(3, 0)
+    arrive(rows_in[3, 1])
     rows_back(2, 0)
     forward(1, 1)
     parts(1, 2)
@@ -369,11 +414,10 @@
     backward(1, 1)
     rows_back(3, 1)
     rows_back(2, 1)
-    rows_back(1, 0)
-    rows_back(1, 1)
-    for columns in HALVES:
-        for m in range(LOCAL):
-            rows_back(0, m, columns)
+    for p in (1, 0):
+        for low, high in ((EARLY, PAIR), (0, EARLY)):
+            for m in range(LOCAL):
+                rows_back(p, m, low, high)
     parts(1, 1)
     parts(1, 3)
     parts(1, 0)
@@ -386,9 +430,17 @@
             start += half * size
         return pl.ds(start, size)
 
-    def returned(p, columns=(0, D)):
-        arrive(back[p, columns])
-        combine(p, columns)
+    def returned(p):
+        arrive(back[p, 0])
+        combine(p, 0, 0, 2 * FRAMES)
+
+    def returned_second(p):
+        arrive(back[p, EARLY])
+        combine(p, EARLY, FRAMES, 2 * FRAMES)
+
+    def returned_first(p):
+        arrive(back[p, 0])
+        combine(p, 0, 0, FRAMES)
 
     returned(3)
     up = send(par.at[chunk(4, 0)], zhalf.at[0], z_up)
@@ -401,33 +453,29 @@
     arrive([down])
     add(par, (chunk(5, 1),), zhalf[1])
     down = send(par.at[chunk(5)], zin.at[1, 0], z_down)
-    returned(1)
+    returned_second(1)
     arrive([up])
     add(par, (chunk(2),), zin[0, 0])
     up = send(par.at[chunk(2)], zin.at[0, 1], z_up)
     arrive([down])
     add(par, (chunk(6),), zin[1, 0])
     down = send(par.at[chunk(6)], zin.at[1, 1], z_down)
-    ends = []
-    for place, columns in enumerate(HALVES):
-        part = pl.ds(*columns)
-        returned(0, columns)
-        if place == 0:
-            arrive([down, up])
-        add(par, (chunk(7), part), zin[1, 1, :, part])
-        ends.append([send(par.at[chunk(7), part], zin.at[1, 2, :, part], z_down)])
-        add(par, (chunk(1), part), zin[0, 1, :, part])
-        ends[-1].append(send(par.at[chunk(1), part], zin.at[0, 2, :, part], z_up))
-    last = []
-    for end, columns in zip(ends, HALVES):
-        part = pl.ds(*columns)
-        arrive(end)
-        total = par[chunk(0), part].astype(F32)
-        total = total + zin[0, 2, :, part].astype(F32) + zin[1, 2, :, part].astype(F32)
-        fin[:, part] = total.astype(BF16)
-        last.append(send(fin.at[:, part], sent_ref.at[:, part], partner))
+    returned_first(1)
+    returned_second(0)
+    arrive([up])
+    add(par, (chunk(1),), zin[0, 1])
+    up = send(par.at[chunk(1)], zin.at[0, 2], z_up_other)
+    arrive([down])
+    add(par, (chunk(7),), zin[1, 1])
+    down = send(par.at[chunk(7)], zin.at[1, 2], z_down_other)
+    returned_first(0)
+    across = send(par.at[chunk(0)], fin, partner)
     reduce_last(1, sums[1])
-    arrive(last)
+    arrive([across, up, down])
+    total = fin[...].astype(F32) + zin[0, 2].astype(F32) + zin[1, 2].astype(F32)
+    sent_ref[...] = total.astype(BF16)
+    for copy in outputs:
+        copy.wait()
     for copy in started:
         copy.wait_send()
 
@@ -461,12 +509,12 @@
         kernel,
         name="relay",
         out_shape=shapes,
-        in_specs=[vmem, vmem, vmem, vmem, anywhere, anywhere],
-        out_specs=(anywhere, vmem, vmem),
+        in_specs=[anywhere] * 6,
+        out_specs=(vmem, anywhere, anywhere),
         scratch_shapes=[
             pltpu.VMEM((2, NZ * FRAMES, D), BF16),
             pltpu.VMEM((NZ, 16, FRAMES), F32),
-            pltpu.VMEM((PAIRS, PLANE * PAIR, 2 * FRAMES), BF16),
+            pltpu.VMEM((PAIRS, PLANE, PAIR, 2 * FRAMES), BF16),
             pltpu.VMEM((PAIRS, LOCAL, NX - 1, 2, PAIR, D), BF16),
             pltpu.VMEM((LOCAL, 2, ROWS, D), BF16),
             pltpu.VMEM((LOCAL, NY, QUARTER, H), BF16),
@@ -474,7 +522,7 @@
             pltpu.VMEM((H, ROWS), BF16),
             pltpu.VMEM((ROWS, H), BF16),
             pltpu.VMEM((LOCAL, ROWS, D), BF16),
-            pltpu.VMEM((PAIRS, PLANE * PAIR, D), BF16),
+            pltpu.VMEM((PAIRS, PLANE, PAIR, D), BF16),
             pltpu.VMEM((NZ * FRAMES, D), BF16),
             pltpu.VMEM((2, FRAMES // 2, D), BF16),
             pltpu.VMEM((2, 3, FRAMES, D), BF16),
@@ -485,9 +533,11 @@
             pltpu.VMEM((LOCAL, 2, QUARTER, H), BF16),
             pltpu.VMEM((LOCAL, 2, H, QUARTER), BF16),
             pltpu.VMEM((FRAMES, D), BF16),
+            pltpu.VMEM((8, FRAMES), jnp.int32),
             pltpu.SemaphoreType.DMA((COPIES,)),
             pltpu.SemaphoreType.DMA((COPIES,)),
             pltpu.SemaphoreType.DMA((LOCAL, 2)),
+            pltpu.SemaphoreType.DMA((4 + 2 * LOCAL,)),
         ],
         compiler_params=pltpu.CompilerParams(
             collective_id=0, has_side_effects=True, vmem_limit_bytes=60 * 2**20

time: 142 us -> 140 us (0.986)
  Pallas kernels: 141 us -> 139 us
    pallas_call x1, Pallas kernels: 138 us -> 137 us  [per_device(): pl.pallas_call(kernel, name='relay', out_shape=shapes, in_specs=[anywhere...]
where the time goes in v3:
time: 140 us
  Pallas kernels  139 us (99%)
    pallas_call x1, Pallas kernels, per_device(): pl.pallas_call(kernel, name='relay', out_shape=shapes, in_specs=[anywhere...  137 us

profile of v3, /device:TPU:1, one launch (start us, length us, event | category | flops | bytes accessed | tf_op | source)
XLA Modules:
  0.0 140.0 jit_solution(12740073164767973179)
XLA Ops:
  0.6 136.9 %relay.1 = (bf16[128,1024]{1,0:T(8,128)(2,1)}, bf16[2,256,768]{2,1,0:T(8,128)(2,1)}, bf16[2,768,256]{2,1,0:T(8,128)(2,1)}) custom-call(s32[8,128]{1,0:T(8,128)} %bitcast.17, f32[8,128]{1,0:T(8,128)} %bitcast.18, bf16[128,1024]{1,0:T(8,128)(2,1)} %bitcast.15, bf16[128,1024]{1,0:T(8,128)(2,1)} %bitcast.16, bf16[2,256,768]{2,1,0:T(8,128)(2,1)} %bitcast.13, ...), custom_call_target="tpu_custom_call" | custom-call | tf_op jit(solution)/shard_map/relay/pallas_call | solution.py:508
  137.5 2.3 %publish.1 = (bf16[128,1024]{1,0:T(8,128)(2,1)}, bf16[2,256,768]{2,1,0:T(8,128)(2,1)}, bf16[2,768,256]{2,1,0:T(8,128)(2,1)}) custom-call(bf16[128,1024]{1,0:T(8,128)(2,1)} %get-tuple-element.9.sent_in, bf16[2,256,768]{2,1,0:T(8,128)(2,1)} %get-tuple-element.10.gi_in, bf16[2,768,256]{2,1,0:T(8,128)(2,1)} %get-tuple-element.11.go_in), custom_call_target="tpu_custom_call" | custom-call | tf_op jit(solution)/shard_map/publish/pallas_call | solution.py:546

commit v4 on v3

--- a/solution.py
+++ b/solution.py
@@ -271,9 +271,6 @@
             scatter(0, m, kind, EARLY)
     up, down = up_next, down_next
     for p, (a, b) in ((1, (6, 2)), (2, (5, 3))):
-        if p == 2:
-            second = [gather_second(0, first[0])]
-            first.append(gather_first(1))
         arrive(down_route)
         arrive(up_route)
         if p == 1:
@@ -288,6 +285,11 @@
             up_next[kind] = hop(a, -1, kind, 0 if p == 2 else None)
             pick(p, kind, slot_gate)
             scatter(p, 0, kind)
+            if p == 1:
+                scatter(p, 1, kind)
+                if kind == 0:
+                    second = [gather_second(0, first[0])]
+                    first.append(gather_first(1))
         up, down = up_next, down_next
     arrive(up_route)
     slot_gate = prepare(3)
@@ -295,7 +297,7 @@
         arrive(down[kind] + up[kind])
         pick(3, kind, slot_gate)
         scatter(3, 0, kind)
-    for p in range(1, PAIRS):
+    for p in (2, 3):
         for kind in range(2):
             scatter(p, 1, kind)
 
@@ -388,15 +390,15 @@
         for p in (2 * c, 2 * c + 1):
             arrive(rows_in[p, 0])
         forward(0, c)
+        if c == 0:
+            second.append(gather_second(1, first[1]))
     parts(0, 2)
     sums = [reduce_first(0)]
-    second.append(gather_second(1, first[1]))
     parts(0, 1)
     parts(0, 3)
     parts(0, 0)
     for c in range(2):
         backward(0, c)
-    sums[0] = reduce_second(0, sums[0])
 
     arrive(second[1])
     own[2].wait()
@@ -404,6 +406,7 @@
     arrive(rows_in[0, 1] + rows_in[1, 1])
     forward(1, 0)
     backward(1, 0)
+    sums[0] = reduce_second(0, sums[0])
     arrive(rows_in[2, 1])
     rows_back(3, 0)
     arrive(rows_in[3, 1])
@@ -471,12 +474,16 @@
     returned_first(0)
     across = send(par.at[chunk(0)], fin, partner)
     reduce_last(1, sums[1])
-    arrive([across, up, down])
+    late = (across, up, down)
+    for copy in started:
+        if all(copy is not other for other in late):
+            copy.wait_send()
+    arrive(late)
     total = fin[...].astype(F32) + zin[0, 2].astype(F32) + zin[1, 2].astype(F32)
     sent_ref[...] = total.astype(BF16)
     for copy in outputs:
         copy.wait()
-    for copy in started:
+    for copy in late:
         copy.wait_send()
 
 

time: 140 us -> 135 us (0.964)
  Pallas kernels: 139 us -> 134 us
    pallas_call x1, Pallas kernels: 137 us -> 131 us  [per_device(): pl.pallas_call(kernel, name='relay', out_shape=shapes, in_specs=[anywhere...]
where the time goes in v4:
time: 135 us; the launch traced here: 134 us
  Pallas kernels  134 us (99%)
    pallas_call x1, Pallas kernels, per_device(): pl.pallas_call(kernel, name='relay', out_shape=shapes, in_specs=[anywhere...  131 us

profile of v4, /device:TPU:1, one launch (start us, length us, event | category | flops | bytes accessed | tf_op | source)
XLA Modules:
  0.0 134.5 jit_solution(7423632919639358711)
XLA Ops:
  0.6 131.4 %relay.1 = (bf16[128,1024]{1,0:T(8,128)(2,1)}, bf16[2,256,768]{2,1,0:T(8,128)(2,1)}, bf16[2,768,256]{2,1,0:T(8,128)(2,1)}) custom-call(s32[8,128]{1,0:T(8,128)} %bitcast.17, f32[8,128]{1,0:T(8,128)} %bitcast.18, bf16[128,1024]{1,0:T(8,128)(2,1)} %bitcast.15, bf16[128,1024]{1,0:T(8,128)(2,1)} %bitcast.16, bf16[2,256,768]{2,1,0:T(8,128)(2,1)} %bitcast.13, ...), custom_call_target="tpu_custom_call" | custom-call | tf_op jit(solution)/shard_map/relay/pallas_call | solution.py:515
  132.0 2.3 %publish.1 = (bf16[128,1024]{1,0:T(8,128)(2,1)}, bf16[2,256,768]{2,1,0:T(8,128)(2,1)}, bf16[2,768,256]{2,1,0:T(8,128)(2,1)}) custom-call(bf16[128,1024]{1,0:T(8,128)(2,1)} %get-tuple-element.9.sent_in, bf16[2,256,768]{2,1,0:T(8,128)(2,1)} %get-tuple-element.10.gi_in, bf16[2,768,256]{2,1,0:T(8,128)(2,1)} %get-tuple-element.11.go_in), custom_call_target="tpu_custom_call" | custom-call | tf_op jit(solution)/shard_map/publish/pallas_call | solution.py:553

commit v5 on v4

--- a/solution.py
+++ b/solution.py
@@ -17,7 +17,8 @@
 CHUNK = ROWS // 2
 QUARTER = D // NY
 TILE = 256
-COPIES = 176
+COPIES = 192
+HALVES = ((0, D // 2), (D // 2, D // 2))
 EARLY = 16
 ORDER = (0, 1, 7, 2, 6, 3, 5, 4)
 SLOT = {distance: place for place, distance in enumerate(ORDER)}
@@ -343,16 +344,26 @@
     def add(ref, place, term):
         ref[place] = (ref[place].astype(F32) + term.astype(F32)).astype(BF16)
 
+    ends = {(m, way): [] for m in range(LOCAL) for way in range(2)}
+
+    def reduce_to(m, way, half, to):
+        j = 1 if way == 0 else 3
+        for part, end, size in ((pi, end_i, half_i), (po, end_o, half_o)):
+            rows = pl.ds(half * size, size)
+            ends[m, way].append(send(part.at[m, j, rows], end.at[m, way, rows], to))
+
+    def reduce_alone(m):
+        for way, to in ((0, y_up), (1, y_down)):
+            reduce_to(m, way, 1 - way, to)
+
     def reduce_second(m, copies):
-        after = []
         for way, to in ((0, y_up), (1, y_down)):
             j = 1 if way == 0 else 3
             arrive(copies[2 * way : 2 * way + 2])
             add(pi, (m, j, pl.ds(way * half_i, half_i)), hop_i[m, way])
             add(po, (m, j, pl.ds(way * half_o, half_o)), hop_o[m, way])
-            after.append(send(pi.at[m, j], end_i.at[m, way], to))
-            after.append(send(po.at[m, j], end_o.at[m, way], to))
-        return after
+            reduce_to(m, way, way, to)
+        return ends[m, 0] + ends[m, 1]
 
     outputs = []
 
@@ -366,18 +377,20 @@
             )
             outputs[-1].start()
 
-    back = {(p, low): [] for p in range(PAIRS) for low in (0, EARLY)}
-
-    def rows_back(p, m, low=0, high=PAIR):
+    back = {}
+
+    def rows_back(p, m, low=0, high=PAIR, columns=(0, D)):
+        part = pl.ds(*columns)
         for b in range(1, NX):
             rows = pl.ds((p * NX + b) * PAIR + low, high - low)
-            place = rr.at[p, (NX - b) * LOCAL + m, pl.ds(low, high - low)]
-            back[p, low].append(send(rg.at[m, rows], place, x_far[b]))
-        rr[p, m, low:high, :] = rg[m, pl.ds(p * NX * PAIR + low, high - low), :]
-
-    def combine(p, low, begin, end):
+            place = rr.at[p, (NX - b) * LOCAL + m, pl.ds(low, high - low), part]
+            copy = send(rg.at[m, rows, part], place, x_far[b])
+            back.setdefault((p, low, columns), []).append(copy)
+        rr[p, m, low:high, part] = rg[m, pl.ds(p * NX * PAIR + low, high - low), part]
+
+    def combine(p, low, begin, end, columns=(0, D)):
         chosen = hot[p, :, low:, begin:end].reshape(PLANE * (PAIR - low), end - begin)
-        for start in range(0, D, TILE):
+        for start in range(columns[0], columns[0] + columns[1], TILE):
             tile = pl.ds(start, TILE)
             rows = rr[p, :, low:, tile].reshape(PLANE * (PAIR - low), TILE)
             total = contract(chosen, rows, 0, 0)
@@ -396,6 +409,7 @@
     sums = [reduce_first(0)]
     parts(0, 1)
     parts(0, 3)
+    reduce_alone(0)
     parts(0, 0)
     for c in range(2):
         backward(0, c)
@@ -410,19 +424,19 @@
     arrive(rows_in[2, 1])
     rows_back(3, 0)
     arrive(rows_in[3, 1])
-    rows_back(2, 0)
     forward(1, 1)
     parts(1, 2)
     sums.append(reduce_first(1))
     backward(1, 1)
     rows_back(3, 1)
-    rows_back(2, 1)
-    for p in (1, 0):
-        for low, high in ((EARLY, PAIR), (0, EARLY)):
+    for p in (2, 1, 0):
+        pieces = [(EARLY, PAIR, columns) for columns in (HALVES if p == 0 else ((0, D),))]
+        for low, high, columns in (*pieces, (0, EARLY, (0, D))):
             for m in range(LOCAL):
-                rows_back(p, m, low, high)
+                rows_back(p, m, low, high, columns)
     parts(1, 1)
     parts(1, 3)
+    reduce_alone(1)
     parts(1, 0)
     reduce_last(0, sums[0])
 
@@ -434,47 +448,51 @@
         return pl.ds(start, size)
 
     def returned(p):
-        arrive(back[p, 0])
+        arrive(back[p, 0, (0, D)])
         combine(p, 0, 0, 2 * FRAMES)
 
-    def returned_second(p):
-        arrive(back[p, EARLY])
-        combine(p, EARLY, FRAMES, 2 * FRAMES)
+    def returned_second(p, columns=(0, D)):
+        arrive(back[p, EARLY, columns])
+        combine(p, EARLY, FRAMES, 2 * FRAMES, columns)
 
     def returned_first(p):
-        arrive(back[p, 0])
+        arrive(back[p, 0, (0, D)])
         combine(p, 0, 0, FRAMES)
+
+    def pass_on(way, distance, step, columns, to):
+        part = pl.ds(*columns)
+        add(par, (chunk(distance), part), zin[way, step, :, part])
+        return send(par.at[chunk(distance), part], zin.at[way, step + 1, :, part], to)
 
     returned(3)
     up = send(par.at[chunk(4, 0)], zhalf.at[0], z_up)
     down = send(par.at[chunk(4, 1)], zhalf.at[1], z_down)
-    sums[1] = reduce_second(1, sums[1])
-    returned(2)
+    returned_second(2)
     arrive([up])
     add(par, (chunk(3, 0),), zhalf[0])
     up = send(par.at[chunk(3)], zin.at[0, 0], z_up)
     arrive([down])
     add(par, (chunk(5, 1),), zhalf[1])
     down = send(par.at[chunk(5)], zin.at[1, 0], z_down)
+    sums[1] = reduce_second(1, sums[1])
+    returned_first(2)
     returned_second(1)
     arrive([up])
-    add(par, (chunk(2),), zin[0, 0])
-    up = send(par.at[chunk(2)], zin.at[0, 1], z_up)
+    up = [pass_on(0, 2, 0, columns, z_up) for columns in HALVES]
     arrive([down])
-    add(par, (chunk(6),), zin[1, 0])
-    down = send(par.at[chunk(6)], zin.at[1, 1], z_down)
+    down = [pass_on(1, 6, 0, columns, z_down) for columns in HALVES]
     returned_first(1)
-    returned_second(0)
-    arrive([up])
-    add(par, (chunk(1),), zin[0, 1])
-    up = send(par.at[chunk(1)], zin.at[0, 2], z_up_other)
-    arrive([down])
-    add(par, (chunk(7),), zin[1, 1])
-    down = send(par.at[chunk(7)], zin.at[1, 2], z_down_other)
+    late = []
+    for half, columns in enumerate(HALVES):
+        arrive([down[half]])
+        late.append(pass_on(1, 7, 1, columns, z_down_other))
+        returned_second(0, columns)
+        arrive([up[half]])
+        late.append(pass_on(0, 1, 1, columns, z_up_other))
     returned_first(0)
     across = send(par.at[chunk(0)], fin, partner)
     reduce_last(1, sums[1])
-    late = (across, up, down)
+    late.append(across)
     for copy in started:
         if all(copy is not other for other in late):
             copy.wait_send()

time: 135 us -> 130 us (0.963)
  Pallas kernels: 134 us -> 129 us
    pallas_call x1, Pallas kernels: 131 us -> 127 us  [per_device(): pl.pallas_call(kernel, name='relay', out_shape=shapes, in_specs=[anywhere...]
where the time goes in v5:
time: 130 us
  Pallas kernels  129 us (99%)
    pallas_call x1, Pallas kernels, per_device(): pl.pallas_call(kernel, name='relay', out_shape=shapes, in_specs=[anywhere...  127 us

profile of v5, /device:TPU:1, one launch (start us, length us, event | category | flops | bytes accessed | tf_op | source)
XLA Modules:
  0.0 129.8 jit_solution(4565459183795475283)
XLA Ops:
  0.6 126.7 %relay.1 = (bf16[128,1024]{1,0:T(8,128)(2,1)}, bf16[2,256,768]{2,1,0:T(8,128)(2,1)}, bf16[2,768,256]{2,1,0:T(8,128)(2,1)}) custom-call(s32[8,128]{1,0:T(8,128)} %bitcast.17, f32[8,128]{1,0:T(8,128)} %bitcast.18, bf16[128,1024]{1,0:T(8,128)(2,1)} %bitcast.15, bf16[128,1024]{1,0:T(8,128)(2,1)} %bitcast.16, bf16[2,256,768]{2,1,0:T(8,128)(2,1)} %bitcast.13, ...), custom_call_target="tpu_custom_call" | custom-call | tf_op jit(solution)/shard_map/relay/pallas_call | solution.py:533
  127.3 2.3 %publish.1 = (bf16[128,1024]{1,0:T(8,128)(2,1)}, bf16[2,256,768]{2,1,0:T(8,128)(2,1)}, bf16[2,768,256]{2,1,0:T(8,128)(2,1)}) custom-call(bf16[128,1024]{1,0:T(8,128)(2,1)} %get-tuple-element.9.sent_in, bf16[2,256,768]{2,1,0:T(8,128)(2,1)} %get-tuple-element.10.gi_in, bf16[2,768,256]{2,1,0:T(8,128)(2,1)} %get-tuple-element.11.go_in), custom_call_target="tpu_custom_call" | custom-call | tf_op jit(solution)/shard_map/publish/pallas_call | solution.py:571

commit v6 on v5

--- a/solution.py
+++ b/solution.py
@@ -437,8 +437,6 @@
     parts(1, 1)
     parts(1, 3)
     reduce_alone(1)
-    parts(1, 0)
-    reduce_last(0, sums[0])
 
     def chunk(distance, half=None):
         start, size = SLOT[distance] * FRAMES, FRAMES
@@ -467,6 +465,8 @@
     returned(3)
     up = send(par.at[chunk(4, 0)], zhalf.at[0], z_up)
     down = send(par.at[chunk(4, 1)], zhalf.at[1], z_down)
+    parts(1, 0)
+    reduce_last(0, sums[0])
     returned_second(2)
     arrive([up])
     add(par, (chunk(3, 0),), zhalf[0])

time: 130 us -> 128 us (0.985)
  Pallas kernels: 129 us -> 127 us
    pallas_call x1, Pallas kernels: 127 us -> 125 us  [per_device(): pl.pallas_call(kernel, name='relay', out_shape=shapes, in_specs=[anywhere...]
where the time goes in v6:
time: 128 us
  Pallas kernels  127 us (99%)
    pallas_call x1, Pallas kernels, per_device(): pl.pallas_call(kernel, name='relay', out_shape=shapes, in_specs=[anywhere...  125 us

profile of v6, /device:TPU:1, one launch (start us, length us, event | category | flops | bytes accessed | tf_op | source)
XLA Modules:
  0.0 128.0 jit_solution(11849890712951130596)
XLA Ops:
  0.6 124.9 %relay.1 = (bf16[128,1024]{1,0:T(8,128)(2,1)}, bf16[2,256,768]{2,1,0:T(8,128)(2,1)}, bf16[2,768,256]{2,1,0:T(8,128)(2,1)}) custom-call(s32[8,128]{1,0:T(8,128)} %bitcast.17, f32[8,128]{1,0:T(8,128)} %bitcast.18, bf16[128,1024]{1,0:T(8,128)(2,1)} %bitcast.15, bf16[128,1024]{1,0:T(8,128)(2,1)} %bitcast.16, bf16[2,256,768]{2,1,0:T(8,128)(2,1)} %bitcast.13, ...), custom_call_target="tpu_custom_call" | custom-call | tf_op jit(solution)/shard_map/relay/pallas_call | solution.py:533
  125.6 2.3 %publish.1 = (bf16[128,1024]{1,0:T(8,128)(2,1)}, bf16[2,256,768]{2,1,0:T(8,128)(2,1)}, bf16[2,768,256]{2,1,0:T(8,128)(2,1)}) custom-call(bf16[128,1024]{1,0:T(8,128)(2,1)} %get-tuple-element.9.sent_in, bf16[2,256,768]{2,1,0:T(8,128)(2,1)} %get-tuple-element.10.gi_in, bf16[2,768,256]{2,1,0:T(8,128)(2,1)} %get-tuple-element.11.go_in), custom_call_target="tpu_custom_call" | custom-call | tf_op jit(solution)/shard_map/publish/pallas_call | solution.py:571

commit v7 on v6

--- a/solution.py
+++ b/solution.py
@@ -425,10 +425,10 @@
     rows_back(3, 0)
     arrive(rows_in[3, 1])
     forward(1, 1)
+    backward(1, 1)
+    rows_back(3, 1)
     parts(1, 2)
     sums.append(reduce_first(1))
-    backward(1, 1)
-    rows_back(3, 1)
     for p in (2, 1, 0):
         pieces = [(EARLY, PAIR, columns) for columns in (HALVES if p == 0 else ((0, D),))]
         for low, high, columns in (*pieces, (0, EARLY, (0, D))):

time: 128 us -> 128 us (level)
  no operation moved by 1% of the time
where the time goes in v7:
time: 128 us
  Pallas kernels  127 us (99%)
    pallas_call x1, Pallas kernels, per_device(): pl.pallas_call(kernel, name='relay', out_shape=shapes, in_specs=[anywhere...  125 us

profile of v7, /device:TPU:1, one launch (start us, length us, event | category | flops | bytes accessed | tf_op | source)
XLA Modules:
  0.0 127.7 jit_solution(3933182685736517491)
XLA Ops:
  0.6 124.6 %relay.1 = (bf16[128,1024]{1,0:T(8,128)(2,1)}, bf16[2,256,768]{2,1,0:T(8,128)(2,1)}, bf16[2,768,256]{2,1,0:T(8,128)(2,1)}) custom-call(s32[8,128]{1,0:T(8,128)} %bitcast.17, f32[8,128]{1,0:T(8,128)} %bitcast.18, bf16[128,1024]{1,0:T(8,128)(2,1)} %bitcast.15, bf16[128,1024]{1,0:T(8,128)(2,1)} %bitcast.16, bf16[2,256,768]{2,1,0:T(8,128)(2,1)} %bitcast.13, ...), custom_call_target="tpu_custom_call" | custom-call | tf_op jit(solution)/shard_map/relay/pallas_call | solution.py:533
  125.2 2.3 %publish.1 = (bf16[128,1024]{1,0:T(8,128)(2,1)}, bf16[2,256,768]{2,1,0:T(8,128)(2,1)}, bf16[2,768,256]{2,1,0:T(8,128)(2,1)}) custom-call(bf16[128,1024]{1,0:T(8,128)(2,1)} %get-tuple-element.9.sent_in, bf16[2,256,768]{2,1,0:T(8,128)(2,1)} %get-tuple-element.10.gi_in, bf16[2,768,256]{2,1,0:T(8,128)(2,1)} %get-tuple-element.11.go_in), custom_call_target="tpu_custom_call" | custom-call | tf_op jit(solution)/shard_map/publish/pallas_call | solution.py:571
